TPU v7x, 512 devices: a whole 4x8x8 slice. The times are simulated.
512 devices in a mesh: section: 128 (over z, y, core), rep: 4 (over x).
Axes of the slice: x: 4, y: 8, z: 8, core: 2. Of those that a mesh axis runs over, the one named last changes fastest.
Arguments:
- node_feats: bfloat16 [32768, 256], P(('section', 'rep')), may hold values from -6 to 6
- weight: bfloat16 [256, 256], replicated, may hold values from -0.375 to 0.375
- node_scale: bfloat16 [32768], P(('section', 'rep')), may hold values from 0.19921875 to 1
- tile_mask: int32 [256, 256], P('section'), may hold values from 0 to 1, as said below
- cotangent: bfloat16 [32768, 256], P(('section', 'rep')), may hold values from -6 to 6
Outputs:
- layer_out: bfloat16 [32768, 256], P(('section', 'rep'))
- grad_feats: bfloat16 [32768, 256], P(('section', 'rep'))
- grad_weight: float32 [256, 256], replicated
Inputs may be any that keep to these rules, and one draw needn't show every extreme that they name: tile_mask is symmetric, 0 or 1, with ones on its diagonal and next to it.
All inputs are finite; a program needn't handle non-finite values.
Results may differ from a plain program's by a relative error of at most 0.0067.
Values may be sent and summed in bfloat16 or wider, within the bound.
A program may use at most 64 MiB of HBM per device.

v0:
```python
import functools
import math

import jax
import jax.numpy as jnp
from jax import lax
from jax.experimental import pallas as pl
from jax.experimental.pallas import tpu as pltpu
from jax.sharding import PartitionSpec as P


MESH = pl.DeviceIdType.MESH
NZ, NY, NX = 8, 8, 4
ROWS = 64
HALF = 128
MODULUS = 65521
OFFSET = (0, 1, 7, 2, 6, 3, 5, 4)
SLOT = {off: k for k, off in enumerate(OFFSET)}
GROUPS = ((0, 1), (1, 3), (3, 5), (5, 8))
COPIES = 160
BF16 = jnp.bfloat16
F32 = jnp.float32


def fold(v):
    return (v & 0xFFFF) + 15 * (v >> 16)


def reduce_once(v):
    return jnp.where(v >= MODULUS, v - MODULUS, v)


def add_mod(q, step):
    total = q + step
    return jnp.where(total >= float(MODULUS), total - float(MODULUS), total)


def kernel(
    coef,
    feats_hbm, weight_hbm, scale_hbm, mask_hbm, cot_hbm,
    layer_out, grad_feats, grad_weight,
    feats, weight, scale_row, mask, cot, load_sems,
    adj, adj_t, cm, cm_low, cm_high, gath, gath_t, masks, csend, crecv, acc, ysend, yrecv,
    near_send, near_recv, keep, keep_near, next_send, next_recv, zsend, zrecv,
    part, a1s, a1r, half, a2s, a2r, a3r, a4r, wbuf, scale_col,
    send_sems, recv_sems,
):
    sec = lax.axis_index("section")
    x = lax.axis_index("rep")
    c = sec % 2
    y = (sec // 2) % NY
    z = sec // (2 * NY)
    x_one = x + 1 - 2 * (x % 2)
    x_two = 3 - x
    x_opp = (x + 2) % NX

    def device(zz, yy, cc, xx):
        return ((zz * NY + yy) * 2 + cc, xx)

    sibling = device(z, y, 1 - c, x)
    east, west = device(z, y, c, x_one), device(z, y, c, x_two)

    def z_peer(e):
        return device((z + e) % NZ, y, c, x)

    def y_peer(e):
        return device(z, (y + e) % NY, c, x)

    def x_peer(e):
        return device(z, y, c, (x + e) % NX)

    barrier = pltpu.get_barrier_semaphore()
    peers = [z_peer(e) for e in range(1, NZ)] + [y_peer(e) for e in range(1, NY)]
    peers += [x_peer(e) for e in range(1, NX)] + [sibling]
    for peer in peers:
        pl.semaphore_signal(barrier, inc=1, device_id=peer, device_id_type=MESH)

    loads = [
        pltpu.make_async_copy(src, dst, load_sems.at[n])
        for n, (src, dst) in enumerate((
            (feats_hbm, feats), (scale_hbm, scale_row), (mask_hbm, mask),
            (weight_hbm, weight), (cot_hbm, cot),
        ))
    ]
    for one in loads:
        one.start()

    started = []

    def copy(src, dst, target):
        number = len(started)
        one = pltpu.make_async_remote_copy(
            src_ref=src, dst_ref=dst, send_sem=send_sems.at[number],
            recv_sem=recv_sems.at[number], device_id=target, device_id_type=MESH,
        )
        one.start()
        started.append(one)
        return one

    for one in loads[:3]:
        one.wait()
    row = scale_row[...].astype(F32)
    pick = lax.broadcasted_iota(jnp.int32, (ROWS, ROWS), 0) == lax.broadcasted_iota(
        jnp.int32, (ROWS, ROWS), 1
    )
    column = jnp.sum(jnp.where(pick, jnp.broadcast_to(row, (ROWS, ROWS)), 0.0), axis=1, keepdims=True)
    scale_col[...] = jnp.broadcast_to(column, (ROWS, 256))
    scaled = (scale_col[...] * feats[...].astype(F32)).astype(BF16)
    gath[0, 0, 0:ROWS] = scaled[:, :HALF]
    gath_t[0, 0, 0:ROWS] = scaled[:, HALF:]
    masks[z] = jnp.zeros((8, HALF), F32)
    masks[z, 0:2, :] = mask[:, 0:HALF].astype(F32)
    masks[z, 2:4, :] = mask[:, HALF:].astype(F32)

    pl.semaphore_wait(barrier, len(peers))

    def start_pass(p):
        own = gath.at[p, 0, pl.ds(0, ROWS)]
        own_t = gath_t.at[p, 0, pl.ds(0, ROWS)]
        state = {"z": {}, "one": {}, "two": {}, "opp": [], "y_t": {}, "core_t": []}
        for k in range(1, NZ):
            e = (NZ - OFFSET[k]) % NZ
            run = pl.ds(k * ROWS, ROWS)
            state["z"][k] = copy(own, gath.at[p, 0, run], z_peer(e))
            state["y_t"][k] = copy(own_t, gath_t.at[p, 0, run], y_peer(e))
            if k == 2:
                forward(p, 0, state)
                forward_t(p, 0, state)
        return state

    def forward_t(p, g, state):
        lo, hi = GROUPS[g]
        for k in range(lo, hi):
            if k:
                state["y_t"][k].wait_recv()
        run = pl.ds(lo * ROWS, (hi - lo) * ROWS)
        state["core_t"].append(copy(gath_t.at[p, 0, run], gath_t.at[p, 1, run], sibling))

    def forward(p, g, state):
        lo, hi = GROUPS[g]
        for k in range(lo, hi):
            if k:
                state["z"][k].wait_recv()
        run = pl.ds(lo * ROWS, (hi - lo) * ROWS)
        state["one"][g] = copy(gath.at[p, 0, run], gath.at[p, 1, run], east)
        state["two"][g] = copy(gath.at[p, 0, run], gath.at[p, 2, run], west)

    def relay(p, g, state):
        lo, hi = GROUPS[g]
        size = (hi - lo) * ROWS // 2
        run = pl.ds(lo * ROWS, size)
        state["two"][g].wait_recv()
        state["opp"].append(copy(gath.at[p, 2, run], gath.at[p, 3, run], east))
        run = pl.ds(lo * ROWS + size, size)
        state["one"][g].wait_recv()
        state["opp"].append(copy(gath.at[p, 1, run], gath.at[p, 3, run], west))

    def finish_gather(state):
        for one in state["opp"]:
            one.wait_recv()

    def product(p, side):
        right = gath[p].reshape(NX * NZ * ROWS, HALF)
        value = jnp.dot(adj[side * 512:(side + 1) * 512, :], right, preferred_element_type=F32)
        if side == 0:
            csend[p] = value.astype(BF16)
        else:
            acc[...] = value

    def sums_first(p, state):
        product(p, 0)
        state["core"] = copy(csend.at[p], crecv.at[p], sibling)

    def sums_second(p, state):
        state["core"].wait_recv()
        total = acc[...] + crecv[p].astype(F32)
        acc[...] = total
        ysend[p] = total.astype(BF16)
        state["y"] = {}
        for e in (4, 3, 5, 2, 6, 1, 7):
            at = pl.multiple_of(((y + e) % NY) * ROWS, ROWS)
            state["y"][e] = copy(ysend.at[p, pl.ds(at, ROWS)], yrecv.at[p, e], y_peer(e))

    def sums_last(p, state):
        total = acc[pl.ds(pl.multiple_of(y * ROWS, ROWS), ROWS), :]
        for e in (1, 7, 2, 6, 3, 5, 4):
            state["y"][e].wait_recv()
            total = total + yrecv[p, e].astype(F32)
        return total

    def product_t(p, lo, hi):
        right = gath_t[p].reshape(2 * NY * ROWS, HALF)
        return jnp.dot(adj_t[lo:hi, :], right, preferred_element_type=F32)

    def near_first(p, state):
        for one in state["core_t"]:
            one.wait_recv()
        opposite = product_t(p, 1536, 2048)
        near_send[p, 0, 256:512] = opposite[:256].astype(BF16)
        near_send[p, 1, 256:512] = opposite[256:].astype(BF16)
        far, close = pl.ds(256, 256), pl.ds(0, 256)
        state["far_e"] = copy(near_send.at[p, 0, far], near_recv.at[p, 0, far], east)
        state["far_w"] = copy(near_send.at[p, 1, far], near_recv.at[p, 1, far], west)
        near_send[p, 0, 0:256] = product_t(p, 512, 768).astype(BF16)
        state["near_e"] = copy(near_send.at[p, 0, close], near_recv.at[p, 0, close], east)
        near_send[p, 1, 0:256] = product_t(p, 1280, 1536).astype(BF16)
        state["near_w"] = copy(near_send.at[p, 1, close], near_recv.at[p, 1, close], west)

    def near_second(p):
        keep_near[0] = product_t(p, 1024, 1280)
        keep_near[1] = product_t(p, 768, 1024)

    def next_first(p, state):
        state["far_e"].wait_recv()
        next_send[p, 0] = (keep_near[0] + near_recv[p, 0, 256:512].astype(F32)).astype(BF16)
        state["next_w"] = copy(next_send.at[p, 0], next_recv.at[p, 0], west)
        state["far_w"].wait_recv()
        next_send[p, 1] = (keep_near[1] + near_recv[p, 1, 256:512].astype(F32)).astype(BF16)
        state["next_e"] = copy(next_send.at[p, 1], next_recv.at[p, 1], east)
        value = product_t(p, 0, 512)
        state["near_e"].wait_recv()
        state["near_w"].wait_recv()
        keep[0:256] = value[:256] + near_recv[p, 0, 0:256].astype(F32)
        keep[256:512] = value[256:] + near_recv[p, 1, 0:256].astype(F32)

    def next_second(p, state):
        state["next_w"].wait_recv()
        state["next_e"].wait_recv()
        total = keep[...] + next_recv[p].reshape(512, HALF).astype(F32)
        keep[...] = total
        zsend[p] = total.astype(BF16)
        state["z_t"] = {}
        for e in (4, 3, 5, 2, 6, 1, 7):
            at = pl.multiple_of(((z + e) % NZ) * ROWS, ROWS)
            state["z_t"][e] = copy(zsend.at[p, pl.ds(at, ROWS)], zrecv.at[p, e], z_peer(e))

    def sums_last_t(p, state):
        total = keep[pl.ds(pl.multiple_of(z * ROWS, ROWS), ROWS), :]
        for e in (1, 7, 2, 6, 3, 5, 4):
            state["z_t"][e].wait_recv()
            total = total + zrecv[p, e].astype(F32)
        return total

    col_j = lax.broadcasted_iota(jnp.int32, (16, 512), 1)
    row_i = lax.broadcasted_iota(jnp.int32, (16, 512), 0)
    col_slot = col_j >> 6
    col_off = jnp.where((col_slot & 1) == 1, (col_slot + 1) >> 1, (8 - (col_slot >> 1)) & 7)
    columns_x = (x, x_one, x_two, x_opp)

    def side_core(side):
        return 1 - c if side == 0 else c

    def mask_columns():
        which = lax.broadcasted_iota(jnp.int32, (16, HALF), 0)
        lane = lax.broadcasted_iota(jnp.int32, (16, HALF), 1)
        core_of = jnp.where(which < 8, 1 - c, c)
        tile = ((z * NY + (which & 7)) * 2 + core_of) * 2 + x // 2
        every = masks[...].reshape(64, HALF)
        dims = (((1,), (1,)), ((), ()))
        low = lax.dot_general((tile == lane).astype(F32), every, dims, preferred_element_type=F32)
        high = lax.dot_general(
            (tile == lane + HALF).astype(F32), every, dims, preferred_element_type=F32
        )
        entry = lax.broadcasted_iota(jnp.int32, (64, 512), 0)
        slot = lax.broadcasted_iota(jnp.int32, (64, 512), 1) >> 6
        off = jnp.where((slot & 1) == 1, (slot + 1) >> 1, (8 - (slot >> 1)) & 7)
        same = (entry >> 3) == ((z + off) & 7)
        for n, xx in enumerate(columns_x):
            pick_low = jnp.where(same & ((entry & 7) == xx // 2), 1.0, 0.0).astype(F32)
            pick_high = jnp.where(same & ((entry & 7) == xx // 2 + 2), 1.0, 0.0).astype(F32)
            chosen = jnp.dot(low, pick_low, preferred_element_type=F32) + jnp.dot(
                high, pick_high, preferred_element_type=F32
            )
            cm[:, n * 512:(n + 1) * 512] = jnp.where(chosen > 0.5, coef, 0.0)

    def mask_columns_t():
        every = masks[...].reshape(64, HALF)
        entry = lax.broadcasted_iota(jnp.int32, (HALF, 512), 0)
        slot = lax.broadcasted_iota(jnp.int32, (HALF, 512), 1) >> 6
        off = jnp.where((slot & 1) == 1, (slot + 1) >> 1, (8 - (slot >> 1)) & 7)
        for h in range(2):
            core_of = c if h == 0 else 1 - c
            tile = ((z * NY + ((y + off) & 7)) * 2 + core_of) * 2 + x // 2
            low = jnp.dot(every, (tile == entry).astype(F32), preferred_element_type=F32)
            high = jnp.dot(every, (tile == entry + HALF).astype(F32), preferred_element_type=F32)
            cm_low[:, h * 512:(h + 1) * 512] = jnp.where(low > 0.5, coef, 0.0)
            cm_high[:, h * 512:(h + 1) * 512] = jnp.where(high > 0.5, coef, 0.0)

    def make(a, b, stride, target, top, lanes, coefs_of):
        first = fold(fold(a * b))
        hashed = reduce_once(fold(fold(first * 20011 + (a + b) * 7919)))
        step = reduce_once(fold(fold(b * 20011 + 7919)))
        step16 = reduce_once(fold(step * 16)).astype(F32)
        leap = reduce_once(fold(step * stride)).astype(F32)

        def run(number, q0):
            coefs = coefs_of(number)
            q = q0
            for s in range(4):
                at = pl.multiple_of(top + number * ROWS + s * 16, 16)
                target[pl.ds(at, 16), lanes] = (
                    (q * (2.0 / 65521.0) - 1.0) * coefs
                ).astype(BF16)
                if s < 3:
                    q = add_mod(q, step16)
            return add_mod(q0, leap)

        lax.fori_loop(0, 8, run, hashed.astype(F32))

    def make_block(n, side):
        b = ((((z + col_off) & 7) * NY + y) * 2 + c) * 256 + columns_x[n] * ROWS + (col_j & 63)
        a = ((z * NY) * 2 + side_core(side)) * 256 + x * ROWS + row_i
        lanes = slice(n * 512, (n + 1) * 512)
        make(a, b, 512, adj, side * 512, lanes, lambda yy: cm[pl.ds(side * 8 + yy, 1), lanes])

    def make_block_t(n, h):
        core_of = c if h == 0 else 1 - c
        b = ((z * NY + ((y + col_off) & 7)) * 2 + core_of) * 256 + x * ROWS + (col_j & 63)
        a = (y * 2 + c) * 256 + columns_x[n] * ROWS + row_i
        lanes = slice(h * 512, (h + 1) * 512)
        tile = columns_x[n] // 2

        def coefs_of(zz):
            low = cm_low[pl.ds(zz * 8 + tile, 1), lanes]
            return low + cm_high[pl.ds(zz * 8 + tile + 2, 1), lanes]

        make(a, b, 4096, adj_t, n * 512, lanes, coefs_of)

    mask_copies = [copy(masks.at[z], masks.at[z], z_peer(e)) for e in range(1, NZ)]
    state = start_pass(0)
    for one in mask_copies:
        one.wait_recv()
    forward(0, 1, state)
    forward_t(0, 1, state)
    relay(0, 0, state)
    mask_columns_t()
    make_block_t(3, 0)
    make_block_t(3, 1)
    forward(0, 2, state)
    forward_t(0, 2, state)
    relay(0, 1, state)
    make_block_t(1, 0)
    make_block_t(1, 1)
    forward(0, 3, state)
    forward_t(0, 3, state)
    relay(0, 2, state)
    make_block_t(2, 0)
    make_block_t(2, 1)
    relay(0, 3, state)
    near_first(0, state)
    near_second(0)
    mask_columns()
    make_block(0, 0)
    make_block(1, 0)
    make_block_t(0, 0)
    make_block_t(0, 1)
    next_first(0, state)
    make_block(2, 0)
    make_block(3, 0)
    finish_gather(state)
    sums_first(0, state)
    for n in range(NX):
        make_block(n, 1)
    product(0, 1)
    next_second(0, state)
    sums_second(0, state)
    sums = jnp.concatenate([sums_last(0, state), sums_last_t(0, state)], axis=1)

    for one in loads[3:]:
        one.wait()
    sums_high = sums.astype(BF16)
    sums_low = (sums - sums_high.astype(F32)).astype(BF16)
    scale = scale_col[...]
    presum = scale * (
        jnp.dot(sums_high, weight[...], preferred_element_type=F32)
        + jnp.dot(sums_low, weight[...], preferred_element_type=F32)
    )
    sigma = jax.nn.sigmoid(presum)
    layer_out[...] = (presum * sigma).astype(BF16)
    deriv = sigma * (1.0 + presum * (1.0 - sigma))
    error = (scale * cot[...].astype(F32) * deriv).astype(BF16)
    gath[1, 0, 0:ROWS] = error[:, :HALF]
    gath_t[1, 0, 0:ROWS] = error[:, HALF:]

    state = start_pass(1)
    part[...] = lax.dot_general(
        sums_high, error, (((0,), (0,)), ((), ())), preferred_element_type=F32
    )
    theirs = pl.multiple_of((1 - c) * 128, 128)
    mine = pl.multiple_of(c * 128, 128)
    a1s[...] = part[pl.ds(theirs, 128), :].astype(BF16)
    first = copy(a1s, a1r, sibling)
    forward(1, 1, state)
    forward_t(1, 1, state)
    relay(1, 0, state)

    first.wait_recv()
    half[...] = part[pl.ds(mine, 128), :] + a1r[...].astype(F32)
    a2s[...] = half[...].astype(BF16)
    second = []
    for e in range(1, NY):
        at = pl.multiple_of(((y + e) % NY) * 16, 16)
        second.append(copy(a2s.at[pl.ds(at, 16)], a2r.at[e], y_peer(e)))

    forward(1, 2, state)
    forward_t(1, 2, state)
    relay(1, 1, state)
    forward(1, 3, state)
    forward_t(1, 3, state)
    relay(1, 2, state)

    piece = half[pl.ds(pl.multiple_of(y * 16, 16), 16), :]
    for e in range(1, NY):
        second[e - 1].wait_recv()
        piece = piece + a2r[e].astype(F32)
    a3r[z] = piece.astype(BF16)
    third = [copy(a3r.at[z], a3r.at[z], z_peer(e)) for e in range(1, NZ)]

    near_first(1, state)
    relay(1, 3, state)
    near_second(1)

    for one in third:
        one.wait_recv()
    piece = a3r[0].astype(F32)
    for n in range(1, NZ):
        piece = piece + a3r[n].astype(F32)
    a4r[x] = piece
    fourth = [copy(a4r.at[x], a4r.at[x], x_peer(e)) for e in range(1, NX)]

    next_first(1, state)
    finish_gather(state)
    sums_first(1, state)
    product(1, 1)

    for one in fourth:
        one.wait_recv()
    piece = (a4r[0] + a4r[1]) + (a4r[2] + a4r[3])
    at = pl.multiple_of(c * 128 + y * 16, 16)
    wbuf[pl.ds(at, 16), :] = piece
    fifth = [copy(wbuf.at[pl.ds(at, 16)], wbuf.at[pl.ds(at, 16)], y_peer(e)) for e in range(1, NY)]

    sums_second(1, state)
    next_second(1, state)
    for one in fifth:
        one.wait_recv()
    sixth = copy(wbuf.at[pl.ds(mine, 128)], wbuf.at[pl.ds(mine, 128)], sibling)
    back = jnp.concatenate([sums_last(1, state), sums_last_t(1, state)], axis=1)
    vgrad = (scale * back).astype(BF16)
    grad_feats[...] = lax.dot_general(
        vgrad, weight[...], (((1,), (1,)), ((), ())), preferred_element_type=F32
    ).astype(BF16)
    sixth.wait_recv()
    grad_weight[...] = wbuf[...]
    for one in started:
        one.wait_send()


def deliver(*refs):
    sems = refs[-1]
    copies = [pltpu.make_async_copy(refs[n], refs[n + 3], sems.at[n]) for n in range(3)]
    for one in copies:
        one.start()
    for one in copies:
        one.wait()


def local(node_feats, weight, node_scale, tile_mask, cotangent, coef):
    hidden = weight.shape[0]
    hbm = pl.BlockSpec(memory_space=pltpu.HBM)
    vmem = pl.BlockSpec(memory_space=pltpu.VMEM)
    shapes = (((ROWS, hidden), BF16), ((ROWS, hidden), BF16), ((hidden, hidden), F32))
    args = (node_feats, weight, node_scale.reshape(1, ROWS), tile_mask, cotangent)
    made = pl.pallas_call(
        functools.partial(kernel, coef),
        out_shape=tuple(pltpu.VMEM(*shape) for shape in shapes),
        in_specs=[hbm] * 5,
        out_specs=(vmem,) * 3,
        scratch_shapes=[
            pltpu.VMEM((ROWS, hidden), BF16),
            pltpu.VMEM((hidden, hidden), BF16),
            pltpu.VMEM((1, ROWS), BF16),
            pltpu.VMEM(tile_mask.shape, jnp.int32),
            pltpu.VMEM((ROWS, hidden), BF16),
            pltpu.SemaphoreType.DMA((5,)),
            pltpu.VMEM((1024, 2048), BF16),
            pltpu.VMEM((2048, 1024), BF16),
            pltpu.VMEM((16, 2048), F32),
            pltpu.VMEM((64, 1024), F32),
            pltpu.VMEM((64, 1024), F32),
            pltpu.VMEM((2, NX, NZ * ROWS, HALF), BF16),
            pltpu.VMEM((2, 2, NY * ROWS, HALF), BF16),
            pltpu.VMEM((NZ, 8, HALF), F32),
            pltpu.VMEM((2, 512, HALF), BF16),
            pltpu.VMEM((2, 512, HALF), BF16),
            pltpu.VMEM((512, HALF), F32),
            pltpu.VMEM((2, 512, HALF), BF16),
            pltpu.VMEM((2, NY, ROWS, HALF), BF16),
            pltpu.VMEM((2, 2, 512, HALF), BF16),
            pltpu.VMEM((2, 2, 512, HALF), BF16),
            pltpu.VMEM((512, HALF), F32),
            pltpu.VMEM((2, 256, HALF), F32),
            pltpu.VMEM((2, 2, 256, HALF), BF16),
            pltpu.VMEM((2, 2, 256, HALF), BF16),
            pltpu.VMEM((2, 512, HALF), BF16),
            pltpu.VMEM((2, NZ, ROWS, HALF), BF16),
            pltpu.VMEM((256, 256), F32),
            pltpu.VMEM((128, 256), BF16),
            pltpu.VMEM((128, 256), BF16),
            pltpu.VMEM((128, 256), F32),
            pltpu.VMEM((128, 256), BF16),
            pltpu.VMEM((NY, 16, 256), BF16),
            pltpu.VMEM((NZ, 16, 256), BF16),
            pltpu.VMEM((NX, 16, 256), F32),
            pltpu.VMEM((256, 256), F32),
            pltpu.VMEM((ROWS, 256), F32),
            pltpu.SemaphoreType.DMA((COPIES,)),
            pltpu.SemaphoreType.DMA((COPIES,)),
        ],
        compiler_params=pltpu.CompilerParams(
            collective_id=0, has_side_effects=True, vmem_limit_bytes=40 * 1024 * 1024
        ),
    )(*(pltpu.with_memory_space_constraint(arg, pltpu.HBM) for arg in args))
    return pl.pallas_call(
        deliver,
        out_shape=tuple(jax.ShapeDtypeStruct(*shape) for shape in shapes),
        in_specs=[vmem] * 3,
        out_specs=(hbm,) * 3,
        scratch_shapes=[pltpu.SemaphoreType.DMA((3,))],
        compiler_params=pltpu.CompilerParams(vmem_limit_bytes=8 * 1024 * 1024),
    )(*(pltpu.with_memory_space_constraint(one, pltpu.VMEM) for one in made))


def solution(mesh):
    in_specs = (
        P(("section", "rep"), None),
        P(),
        P(("section", "rep")),
        P("section", None),
        P(("section", "rep"), None),
    )
    out_specs = (P(("section", "rep"), None), P(("section", "rep"), None), P())
    coef = 4.0 / math.sqrt(128 * 256)
    return jax.shard_map(
        functools.partial(local, coef=coef), mesh=mesh, in_specs=in_specs, out_specs=out_specs,
        check_vma=False,
    )
```

profile of v0, /device:TPU:1, one launch (start us, length us, event | category | flops | bytes accessed | tf_op | source)
XLA Modules:
  0.0 74.4 jit_solution(6526405616342033513)
XLA Ops:
  0.6 73.0 %shard_map.76 = (bf16[64,256]{1,0:T(8,128)(2,1)S(1)}, bf16[64,256]{1,0:T(8,128)(2,1)S(1)}, f32[256,256]{1,0:T(8,128)S(1)}) custom-call(bf16[64,256]{1,0:T(8,128)(2,1)} %feats_hbm.1, bf16[256,256]{1,0:T(8,128)(2,1)} %weight_hbm.1, bf16[1,64]{1,0:T(2,128)(2,1)} %bitcast.1, s32[2,256]{1,0:T(2,128)} %mask_hbm.1, bf16[64,256]{1,0:T(8,128)(2,1)} %cot_hbm.1), custom_call_target="tpu_custom_call" | custom-call | tf_op jit(solution)/shard_map/pallas_call | solution.py:474
  73.6 0.8 %shard_map.77 = (bf16[64,256]{1,0:T(8,128)(2,1)}, bf16[64,256]{1,0:T(8,128)(2,1)}, f32[256,256]{1,0:T(8,128)}) custom-call(bf16[64,256]{1,0:T(8,128)(2,1)S(1)} %get-tuple-element.6.refs_0_, bf16[64,256]{1,0:T(8,128)(2,1)S(1)} %get-tuple-element.7.refs_1_, f32[256,256]{1,0:T(8,128)S(1)} %get-tuple-element.8.refs_2_), custom_call_target="tpu_custom_call" | custom-call | tf_op jit(solution)/shard_map/pallas_call | solution.py:524
where the time goes:
time: 74.5 us; the launch traced here: 74.4 us
  Pallas kernels  73.8 us (99%)
    pallas_call x1, Pallas kernels, local(): pl.pallas_call(functools.partial(kernel, coef), out_shape=tuple((pltpu.VM...  73 us

commit v1 on v0

--- a/solution.py
+++ b/solution.py
@@ -30,9 +30,13 @@
     return jnp.where(v >= MODULUS, v - MODULUS, v)
 
 
-def add_mod(q, step):
-    total = q + step
-    return jnp.where(total >= float(MODULUS), total - float(MODULUS), total)
+SCALE = 2.0 / MODULUS
+WRAP = 1.0 - 0.5 * SCALE
+
+
+def add_wrapped(u, step):
+    total = u + step
+    return jnp.where(total >= WRAP, total - 2.0, total)
 
 
 def kernel(
@@ -42,7 +46,7 @@
     feats, weight, scale_row, mask, cot, load_sems,
     adj, adj_t, cm, cm_low, cm_high, gath, gath_t, masks, csend, crecv, acc, ysend, yrecv,
     near_send, near_recv, keep, keep_near, next_send, next_recv, zsend, zrecv,
-    part, a1s, a1r, half, a2s, a2r, a3r, a4r, wbuf, scale_col,
+    starts, steps, part, a1s, a1r, half, a2s, a2r, a3r, a4r, wbuf, scale_col,
     send_sems, recv_sems,
 ):
     sec = lax.axis_index("section")
@@ -69,12 +73,6 @@
     def x_peer(e):
         return device(z, y, c, (x + e) % NX)
 
-    barrier = pltpu.get_barrier_semaphore()
-    peers = [z_peer(e) for e in range(1, NZ)] + [y_peer(e) for e in range(1, NY)]
-    peers += [x_peer(e) for e in range(1, NX)] + [sibling]
-    for peer in peers:
-        pl.semaphore_signal(barrier, inc=1, device_id=peer, device_id_type=MESH)
-
     loads = [
         pltpu.make_async_copy(src, dst, load_sems.at[n])
         for n, (src, dst) in enumerate((
@@ -85,6 +83,12 @@
     for one in loads:
         one.start()
 
+    barrier = pltpu.get_barrier_semaphore()
+    peers = [z_peer(e) for e in range(1, NZ)] + [y_peer(e) for e in range(1, NY)]
+    peers += [x_peer(e) for e in range(1, NX)] + [sibling]
+    for peer in peers:
+        pl.semaphore_signal(barrier, inc=1, device_id=peer, device_id_type=MESH)
+
     started = []
 
     def copy(src, dst, target):
@@ -96,150 +100,6 @@
         one.start()
         started.append(one)
         return one
-
-    for one in loads[:3]:
-        one.wait()
-    row = scale_row[...].astype(F32)
-    pick = lax.broadcasted_iota(jnp.int32, (ROWS, ROWS), 0) == lax.broadcasted_iota(
-        jnp.int32, (ROWS, ROWS), 1
-    )
-    column = jnp.sum(jnp.where(pick, jnp.broadcast_to(row, (ROWS, ROWS)), 0.0), axis=1, keepdims=True)
-    scale_col[...] = jnp.broadcast_to(column, (ROWS, 256))
-    scaled = (scale_col[...] * feats[...].astype(F32)).astype(BF16)
-    gath[0, 0, 0:ROWS] = scaled[:, :HALF]
-    gath_t[0, 0, 0:ROWS] = scaled[:, HALF:]
-    masks[z] = jnp.zeros((8, HALF), F32)
-    masks[z, 0:2, :] = mask[:, 0:HALF].astype(F32)
-    masks[z, 2:4, :] = mask[:, HALF:].astype(F32)
-
-    pl.semaphore_wait(barrier, len(peers))
-
-    def start_pass(p):
-        own = gath.at[p, 0, pl.ds(0, ROWS)]
-        own_t = gath_t.at[p, 0, pl.ds(0, ROWS)]
-        state = {"z": {}, "one": {}, "two": {}, "opp": [], "y_t": {}, "core_t": []}
-        for k in range(1, NZ):
-            e = (NZ - OFFSET[k]) % NZ
-            run = pl.ds(k * ROWS, ROWS)
-            state["z"][k] = copy(own, gath.at[p, 0, run], z_peer(e))
-            state["y_t"][k] = copy(own_t, gath_t.at[p, 0, run], y_peer(e))
-            if k == 2:
-                forward(p, 0, state)
-                forward_t(p, 0, state)
-        return state
-
-    def forward_t(p, g, state):
-        lo, hi = GROUPS[g]
-        for k in range(lo, hi):
-            if k:
-                state["y_t"][k].wait_recv()
-        run = pl.ds(lo * ROWS, (hi - lo) * ROWS)
-        state["core_t"].append(copy(gath_t.at[p, 0, run], gath_t.at[p, 1, run], sibling))
-
-    def forward(p, g, state):
-        lo, hi = GROUPS[g]
-        for k in range(lo, hi):
-            if k:
-                state["z"][k].wait_recv()
-        run = pl.ds(lo * ROWS, (hi - lo) * ROWS)
-        state["one"][g] = copy(gath.at[p, 0, run], gath.at[p, 1, run], east)
-        state["two"][g] = copy(gath.at[p, 0, run], gath.at[p, 2, run], west)
-
-    def relay(p, g, state):
-        lo, hi = GROUPS[g]
-        size = (hi - lo) * ROWS // 2
-        run = pl.ds(lo * ROWS, size)
-        state["two"][g].wait_recv()
-        state["opp"].append(copy(gath.at[p, 2, run], gath.at[p, 3, run], east))
-        run = pl.ds(lo * ROWS + size, size)
-        state["one"][g].wait_recv()
-        state["opp"].append(copy(gath.at[p, 1, run], gath.at[p, 3, run], west))
-
-    def finish_gather(state):
-        for one in state["opp"]:
-            one.wait_recv()
-
-    def product(p, side):
-        right = gath[p].reshape(NX * NZ * ROWS, HALF)
-        value = jnp.dot(adj[side * 512:(side + 1) * 512, :], right, preferred_element_type=F32)
-        if side == 0:
-            csend[p] = value.astype(BF16)
-        else:
-            acc[...] = value
-
-    def sums_first(p, state):
-        product(p, 0)
-        state["core"] = copy(csend.at[p], crecv.at[p], sibling)
-
-    def sums_second(p, state):
-        state["core"].wait_recv()
-        total = acc[...] + crecv[p].astype(F32)
-        acc[...] = total
-        ysend[p] = total.astype(BF16)
-        state["y"] = {}
-        for e in (4, 3, 5, 2, 6, 1, 7):
-            at = pl.multiple_of(((y + e) % NY) * ROWS, ROWS)
-            state["y"][e] = copy(ysend.at[p, pl.ds(at, ROWS)], yrecv.at[p, e], y_peer(e))
-
-    def sums_last(p, state):
-        total = acc[pl.ds(pl.multiple_of(y * ROWS, ROWS), ROWS), :]
-        for e in (1, 7, 2, 6, 3, 5, 4):
-            state["y"][e].wait_recv()
-            total = total + yrecv[p, e].astype(F32)
-        return total
-
-    def product_t(p, lo, hi):
-        right = gath_t[p].reshape(2 * NY * ROWS, HALF)
-        return jnp.dot(adj_t[lo:hi, :], right, preferred_element_type=F32)
-
-    def near_first(p, state):
-        for one in state["core_t"]:
-            one.wait_recv()
-        opposite = product_t(p, 1536, 2048)
-        near_send[p, 0, 256:512] = opposite[:256].astype(BF16)
-        near_send[p, 1, 256:512] = opposite[256:].astype(BF16)
-        far, close = pl.ds(256, 256), pl.ds(0, 256)
-        state["far_e"] = copy(near_send.at[p, 0, far], near_recv.at[p, 0, far], east)
-        state["far_w"] = copy(near_send.at[p, 1, far], near_recv.at[p, 1, far], west)
-        near_send[p, 0, 0:256] = product_t(p, 512, 768).astype(BF16)
-        state["near_e"] = copy(near_send.at[p, 0, close], near_recv.at[p, 0, close], east)
-        near_send[p, 1, 0:256] = product_t(p, 1280, 1536).astype(BF16)
-        state["near_w"] = copy(near_send.at[p, 1, close], near_recv.at[p, 1, close], west)
-
-    def near_second(p):
-        keep_near[0] = product_t(p, 1024, 1280)
-        keep_near[1] = product_t(p, 768, 1024)
-
-    def next_first(p, state):
-        state["far_e"].wait_recv()
-        next_send[p, 0] = (keep_near[0] + near_recv[p, 0, 256:512].astype(F32)).astype(BF16)
-        state["next_w"] = copy(next_send.at[p, 0], next_recv.at[p, 0], west)
-        state["far_w"].wait_recv()
-        next_send[p, 1] = (keep_near[1] + near_recv[p, 1, 256:512].astype(F32)).astype(BF16)
-        state["next_e"] = copy(next_send.at[p, 1], next_recv.at[p, 1], east)
-        value = product_t(p, 0, 512)
-        state["near_e"].wait_recv()
-        state["near_w"].wait_recv()
-        keep[0:256] = value[:256] + near_recv[p, 0, 0:256].astype(F32)
-        keep[256:512] = value[256:] + near_recv[p, 1, 0:256].astype(F32)
-
-    def next_second(p, state):
-        state["next_w"].wait_recv()
-        state["next_e"].wait_recv()
-        total = keep[...] + next_recv[p].reshape(512, HALF).astype(F32)
-        keep[...] = total
-        zsend[p] = total.astype(BF16)
-        state["z_t"] = {}
-        for e in (4, 3, 5, 2, 6, 1, 7):
-            at = pl.multiple_of(((z + e) % NZ) * ROWS, ROWS)
-            state["z_t"][e] = copy(zsend.at[p, pl.ds(at, ROWS)], zrecv.at[p, e], z_peer(e))
-
-    def sums_last_t(p, state):
-        total = keep[pl.ds(pl.multiple_of(z * ROWS, ROWS), ROWS), :]
-        for e in (1, 7, 2, 6, 3, 5, 4):
-            state["z_t"][e].wait_recv()
-            total = total + zrecv[p, e].astype(F32)
-        return total
 
     col_j = lax.broadcasted_iota(jnp.int32, (16, 512), 1)
     row_i = lax.broadcasted_iota(jnp.int32, (16, 512), 0)
@@ -286,37 +146,60 @@
             cm_low[:, h * 512:(h + 1) * 512] = jnp.where(low > 0.5, coef, 0.0)
             cm_high[:, h * 512:(h + 1) * 512] = jnp.where(high > 0.5, coef, 0.0)
 
-    def make(a, b, stride, target, top, lanes, coefs_of):
+    def column_ids(n):
+        return ((((z + col_off) & 7) * NY + y) * 2 + c) * 256 + columns_x[n] * ROWS + (col_j & 63)
+
+    def column_ids_t(h):
+        core_of = c if h == 0 else 1 - c
+        return ((z * NY + ((y + col_off) & 7)) * 2 + core_of) * 256 + x * ROWS + (col_j & 63)
+
+    def prepare(unit, a, b):
         first = fold(fold(a * b))
         hashed = reduce_once(fold(fold(first * 20011 + (a + b) * 7919)))
-        step = reduce_once(fold(fold(b * 20011 + 7919)))
-        step16 = reduce_once(fold(step * 16)).astype(F32)
-        leap = reduce_once(fold(step * stride)).astype(F32)
-
-        def run(number, q0):
-            coefs = coefs_of(number)
-            q = q0
+        starts[unit] = hashed.astype(F32) * SCALE - 1.0
+
+    def prepare_steps(number, b, stride):
+        step = reduce_once(fold(fold(b[0:8] * 20011 + 7919)))
+        steps[number, 0] = reduce_once(fold(step * 16)).astype(F32) * SCALE
+        steps[number, 1] = reduce_once(fold(step * stride)).astype(F32) * SCALE
+
+    def prepare_block():
+        for n in range(NX):
+            b = column_ids(n)
+            prepare_steps(n, b, 512)
+            for side in range(2):
+                a = ((z * NY) * 2 + side_core(side)) * 256 + x * ROWS + row_i
+                prepare(n * 2 + side, a, b)
+
+    def prepare_block_t():
+        for h in range(2):
+            b = column_ids_t(h)
+            prepare_steps(NX + h, b, 4096)
+            for n in range(NX):
+                a = (y * 2 + c) * 256 + columns_x[n] * ROWS + row_i
+                prepare(8 + n * 2 + h, a, b)
+
+    def make(unit, number, target, top, lanes, coefs_of):
+        step16 = jnp.concatenate([steps[number, 0]] * 2, axis=0)
+        leap = jnp.concatenate([steps[number, 1]] * 2, axis=0)
+
+        def run(turn, u0):
+            coefs = coefs_of(turn)
+            u = u0
             for s in range(4):
-                at = pl.multiple_of(top + number * ROWS + s * 16, 16)
-                target[pl.ds(at, 16), lanes] = (
-                    (q * (2.0 / 65521.0) - 1.0) * coefs
-                ).astype(BF16)
+                at = pl.multiple_of(top + turn * ROWS + s * 16, 16)
+                target[pl.ds(at, 16), lanes] = (u * coefs).astype(BF16)
                 if s < 3:
-                    q = add_mod(q, step16)
-            return add_mod(q0, leap)
-
-        lax.fori_loop(0, 8, run, hashed.astype(F32))
+                    u = add_wrapped(u, step16)
+            return add_wrapped(u0, leap)
+
+        lax.fori_loop(0, 8, run, starts[unit])
 
     def make_block(n, side):
-        b = ((((z + col_off) & 7) * NY + y) * 2 + c) * 256 + columns_x[n] * ROWS + (col_j & 63)
-        a = ((z * NY) * 2 + side_core(side)) * 256 + x * ROWS + row_i
         lanes = slice(n * 512, (n + 1) * 512)
-        make(a, b, 512, adj, side * 512, lanes, lambda yy: cm[pl.ds(side * 8 + yy, 1), lanes])
+        make(n * 2 + side, n, adj, side * 512, lanes, lambda yy: cm[pl.ds(side * 8 + yy, 1), lanes])
 
     def make_block_t(n, h):
-        core_of = c if h == 0 else 1 - c
-        b = ((z * NY + ((y + col_off) & 7)) * 2 + core_of) * 256 + x * ROWS + (col_j & 63)
-        a = (y * 2 + c) * 256 + columns_x[n] * ROWS + row_i
         lanes = slice(h * 512, (h + 1) * 512)
         tile = columns_x[n] // 2
 
@@ -324,10 +207,157 @@
             low = cm_low[pl.ds(zz * 8 + tile, 1), lanes]
             return low + cm_high[pl.ds(zz * 8 + tile + 2, 1), lanes]
 
-        make(a, b, 4096, adj_t, n * 512, lanes, coefs_of)
+        make(8 + n * 2 + h, NX + h, adj_t, n * 512, lanes, coefs_of)
+
+    prepare_block_t()
+
+    for one in loads[:3]:
+        one.wait()
+    row = scale_row[...].astype(F32)
+    pick = lax.broadcasted_iota(jnp.int32, (ROWS, ROWS), 0) == lax.broadcasted_iota(
+        jnp.int32, (ROWS, ROWS), 1
+    )
+    column = jnp.sum(jnp.where(pick, jnp.broadcast_to(row, (ROWS, ROWS)), 0.0), axis=1, keepdims=True)
+    scale_col[...] = jnp.broadcast_to(column, (ROWS, 256))
+    scaled = (scale_col[...] * feats[...].astype(F32)).astype(BF16)
+    gath[0, 0, 0:ROWS] = scaled[:, :HALF]
+    gath_t[0, 0, 0:ROWS] = scaled[:, HALF:]
+    masks[z] = jnp.zeros((8, HALF), F32)
+    masks[z, 0:2, :] = mask[:, 0:HALF].astype(F32)
+    masks[z, 2:4, :] = mask[:, HALF:].astype(F32)
+
+    pl.semaphore_wait(barrier, len(peers))
+
+    def start_pass(p):
+        own = gath.at[p, 0, pl.ds(0, ROWS)]
+        own_t = gath_t.at[p, 0, pl.ds(0, ROWS)]
+        state = {"z": {}, "one": {}, "two": {}, "opp": [], "y_t": {}, "core_t": []}
+        for k in range(1, NZ):
+            e = (NZ - OFFSET[k]) % NZ
+            run = pl.ds(k * ROWS, ROWS)
+            state["z"][k] = copy(own, gath.at[p, 0, run], z_peer(e))
+            state["y_t"][k] = copy(own_t, gath_t.at[p, 0, run], y_peer(e))
+            if k == 2:
+                forward(p, 0, state)
+                forward_t(p, 0, state)
+        return state
+
+    def forward_t(p, g, state):
+        lo, hi = GROUPS[g]
+        for k in range(lo, hi):
+            if k:
+                state["y_t"][k].wait_recv()
+        run = pl.ds(lo * ROWS, (hi - lo) * ROWS)
+        state["core_t"].append(copy(gath_t.at[p, 0, run], gath_t.at[p, 1, run], sibling))
+
+    def forward(p, g, state):
+        lo, hi = GROUPS[g]
+        for k in range(lo, hi):
+            if k:
+                state["z"][k].wait_recv()
+        run = pl.ds(lo * ROWS, (hi - lo) * ROWS)
+        state["one"][g] = copy(gath.at[p, 0, run], gath.at[p, 1, run], east)
+        state["two"][g] = copy(gath.at[p, 0, run], gath.at[p, 2, run], west)
+
+    def relay(p, g, state):
+        lo, hi = GROUPS[g]
+        size = (hi - lo) * ROWS // 2
+        run = pl.ds(lo * ROWS, size)
+        state["two"][g].wait_recv()
+        state["opp"].append(copy(gath.at[p, 2, run], gath.at[p, 3, run], east))
+        run = pl.ds(lo * ROWS + size, size)
+        state["one"][g].wait_recv()
+        state["opp"].append(copy(gath.at[p, 1, run], gath.at[p, 3, run], west))
+
+    def finish_gather(state):
+        for one in state["opp"]:
+            one.wait_recv()
+
+    def product(p, side):
+        right = gath[p].reshape(NX * NZ * ROWS, HALF)
+        value = jnp.dot(adj[side * 512:(side + 1) * 512, :], right, preferred_element_type=F32)
+        if side == 0:
+            csend[p] = value.astype(BF16)
+        else:
+            acc[...] = value
+
+    def sums_first(p, state):
+        product(p, 0)
+        state["core"] = copy(csend.at[p], crecv.at[p], sibling)
+
+    def sums_second(p, state):
+        state["core"].wait_recv()
+        total = acc[...] + crecv[p].astype(F32)
+        acc[...] = total
+        ysend[p] = total.astype(BF16)
+        state["y"] = {}
+        for e in (4, 3, 5, 2, 6, 1, 7):
+            at = pl.multiple_of(((y + e) % NY) * ROWS, ROWS)
+            state["y"][e] = copy(ysend.at[p, pl.ds(at, ROWS)], yrecv.at[p, e], y_peer(e))
+
+    def sums_last(p, state):
+        total = acc[pl.ds(pl.multiple_of(y * ROWS, ROWS), ROWS), :]
+        for e in (1, 7, 2, 6, 3, 5, 4):
+            state["y"][e].wait_recv()
+            total = total + yrecv[p, e].astype(F32)
+        return total
+
+    def product_t(p, lo, hi):
+        right = gath_t[p].reshape(2 * NY * ROWS, HALF)
+        return jnp.dot(adj_t[lo:hi, :], right, preferred_element_type=F32)
+
+    def near_first(p, state):
+        for one in state["core_t"]:
+            one.wait_recv()
+        opposite = product_t(p, 1536, 2048)
+        near_send[p, 0, 256:512] = opposite[:256].astype(BF16)
+        near_send[p, 1, 256:512] = opposite[256:].astype(BF16)
+        far, close = pl.ds(256, 256), pl.ds(0, 256)
+        state["far_e"] = copy(near_send.at[p, 0, far], near_recv.at[p, 0, far], east)
+        state["far_w"] = copy(near_send.at[p, 1, far], near_recv.at[p, 1, far], west)
+        near_send[p, 0, 0:256] = product_t(p, 512, 768).astype(BF16)
+        state["near_e"] = copy(near_send.at[p, 0, close], near_recv.at[p, 0, close], east)
+        near_send[p, 1, 0:256] = product_t(p, 1280, 1536).astype(BF16)
+        state["near_w"] = copy(near_send.at[p, 1, close], near_recv.at[p, 1, close], west)
+
+    def near_second(p):
+        keep_near[0] = product_t(p, 1024, 1280)
+        keep_near[1] = product_t(p, 768, 1024)
+
+    def next_first(p, state):
+        state["far_e"].wait_recv()
+        next_send[p, 0] = (keep_near[0] + near_recv[p, 0, 256:512].astype(F32)).astype(BF16)
+        state["next_w"] = copy(next_send.at[p, 0], next_recv.at[p, 0], west)
+        state["far_w"].wait_recv()
+        next_send[p, 1] = (keep_near[1] + near_recv[p, 1, 256:512].astype(F32)).astype(BF16)
+        state["next_e"] = copy(next_send.at[p, 1], next_recv.at[p, 1], east)
+        value = product_t(p, 0, 512)
+        state["near_e"].wait_recv()
+        state["near_w"].wait_recv()
+        keep[0:256] = value[:256] + near_recv[p, 0, 0:256].astype(F32)
+        keep[256:512] = value[256:] + near_recv[p, 1, 0:256].astype(F32)
+
+    def next_second(p, state):
+        state["next_w"].wait_recv()
+        state["next_e"].wait_recv()
+        total = keep[...] + next_recv[p].reshape(512, HALF).astype(F32)
+        keep[...] = total
+        zsend[p] = total.astype(BF16)
+        state["z_t"] = {}
+        for e in (4, 3, 5, 2, 6, 1, 7):
+            at = pl.multiple_of(((z + e) % NZ) * ROWS, ROWS)
+            state["z_t"][e] = copy(zsend.at[p, pl.ds(at, ROWS)], zrecv.at[p, e], z_peer(e))
+
+    def sums_last_t(p, state):
+        total = keep[pl.ds(pl.multiple_of(z * ROWS, ROWS), ROWS), :]
+        for e in (1, 7, 2, 6, 3, 5, 4):
+            state["z_t"][e].wait_recv()
+            total = total + zrecv[p, e].astype(F32)
+        return total
 
     mask_copies = [copy(masks.at[z], masks.at[z], z_peer(e)) for e in range(1, NZ)]
     state = start_pass(0)
+    prepare_block()
     for one in mask_copies:
         one.wait_recv()
     forward(0, 1, state)
@@ -341,29 +371,30 @@
     relay(0, 1, state)
     make_block_t(1, 0)
     make_block_t(1, 1)
+    make_block_t(2, 0)
     forward(0, 3, state)
     forward_t(0, 3, state)
     relay(0, 2, state)
-    make_block_t(2, 0)
     make_block_t(2, 1)
+    mask_columns()
+    for n in range(3):
+        make_block(n, 0)
+    near_first(0, state)
     relay(0, 3, state)
-    near_first(0, state)
     near_second(0)
-    mask_columns()
-    make_block(0, 0)
-    make_block(1, 0)
+    make_block(3, 0)
     make_block_t(0, 0)
     make_block_t(0, 1)
+    make_block(0, 1)
+    make_block(1, 1)
     next_first(0, state)
-    make_block(2, 0)
-    make_block(3, 0)
     finish_gather(state)
     sums_first(0, state)
-    for n in range(NX):
-        make_block(n, 1)
+    make_block(2, 1)
+    make_block(3, 1)
     product(0, 1)
+    sums_second(0, state)
     next_second(0, state)
-    sums_second(0, state)
     sums = jnp.concatenate([sums_last(0, state), sums_last_t(0, state)], axis=1)
 
     for one in loads[3:]:
@@ -437,7 +468,7 @@
         one.wait_recv()
     piece = (a4r[0] + a4r[1]) + (a4r[2] + a4r[3])
     at = pl.multiple_of(c * 128 + y * 16, 16)
-    wbuf[pl.ds(at, 16), :] = piece
+    wbuf[pl.ds(at, 16), :] = piece.astype(BF16)
     fifth = [copy(wbuf.at[pl.ds(at, 16)], wbuf.at[pl.ds(at, 16)], y_peer(e)) for e in range(1, NY)]
 
     sums_second(1, state)
@@ -451,7 +482,7 @@
         vgrad, weight[...], (((1,), (1,)), ((), ())), preferred_element_type=F32
     ).astype(BF16)
     sixth.wait_recv()
-    grad_weight[...] = wbuf[...]
+    grad_weight[...] = wbuf[...].astype(F32)
     for one in started:
         one.wait_send()
 
@@ -504,6 +535,8 @@
             pltpu.VMEM((2, 2, 256, HALF), BF16),
             pltpu.VMEM((2, 512, HALF), BF16),
             pltpu.VMEM((2, NZ, ROWS, HALF), BF16),
+            pltpu.VMEM((16, 16, 512), F32),
+            pltpu.VMEM((NX + 2, 2, 8, 512), F32),
             pltpu.VMEM((256, 256), F32),
             pltpu.VMEM((128, 256), BF16),
             pltpu.VMEM((128, 256), BF16),
@@ -512,7 +545,7 @@
             pltpu.VMEM((NY, 16, 256), BF16),
             pltpu.VMEM((NZ, 16, 256), BF16),
             pltpu.VMEM((NX, 16, 256), F32),
-            pltpu.VMEM((256, 256), F32),
+            pltpu.VMEM((256, 256), BF16),
             pltpu.VMEM((ROWS, 256), F32),
             pltpu.SemaphoreType.DMA((COPIES,)),
             pltpu.SemaphoreType.DMA((COPIES,)),

time: 74.5 us -> 71.7 us (0.962)
  Pallas kernels: 73.8 us -> 70.9 us
    pallas_call x1, Pallas kernels: 73 us -> 70.2 us  [local(): pl.pallas_call(functools.partial(kernel, coef), out_shape=tuple((pltpu.VM...]
where the time goes in v1:
time: 71.7 us; the launch traced here: 71.6 us
  Pallas kernels  70.9 us (99%)
    pallas_call x1, Pallas kernels, local(): pl.pallas_call(functools.partial(kernel, coef), out_shape=tuple((pltpu.VM...  70.2 us

profile of v1, /device:TPU:1, one launch (start us, length us, event | category | flops | bytes accessed | tf_op | source)
XLA Modules:
  0.0 71.6 jit_solution(16047761401731900570)
XLA Ops:
  0.6 70.2 %shard_map.76 = (bf16[64,256]{1,0:T(8,128)(2,1)S(1)}, bf16[64,256]{1,0:T(8,128)(2,1)S(1)}, f32[256,256]{1,0:T(8,128)S(1)}) custom-call(bf16[64,256]{1,0:T(8,128)(2,1)} %feats_hbm.1, bf16[256,256]{1,0:T(8,128)(2,1)} %weight_hbm.1, bf16[1,64]{1,0:T(2,128)(2,1)} %bitcast.1, s32[2,256]{1,0:T(2,128)} %mask_hbm.1, bf16[64,256]{1,0:T(8,128)(2,1)} %cot_hbm.1), custom_call_target="tpu_custom_call" | custom-call | tf_op jit(solution)/shard_map/pallas_call | solution.py:505
  70.8 0.8 %shard_map.77 = (bf16[64,256]{1,0:T(8,128)(2,1)}, bf16[64,256]{1,0:T(8,128)(2,1)}, f32[256,256]{1,0:T(8,128)}) custom-call(bf16[64,256]{1,0:T(8,128)(2,1)S(1)} %get-tuple-element.6.refs_0_, bf16[64,256]{1,0:T(8,128)(2,1)S(1)} %get-tuple-element.7.refs_1_, f32[256,256]{1,0:T(8,128)S(1)} %get-tuple-element.8.refs_2_), custom_call_target="tpu_custom_call" | custom-call | tf_op jit(solution)/shard_map/pallas_call | solution.py:557

commit v2 on v1

--- a/solution.py
+++ b/solution.py
@@ -16,7 +16,7 @@
 MODULUS = 65521
 OFFSET = (0, 1, 7, 2, 6, 3, 5, 4)
 SLOT = {off: k for k, off in enumerate(OFFSET)}
-GROUPS = ((0, 1), (1, 3), (3, 5), (5, 8))
+GROUPS = ((0, 1), (1, 5), (5, 8))
 COPIES = 160
 BF16 = jnp.bfloat16
 F32 = jnp.float32
@@ -46,7 +46,7 @@
     feats, weight, scale_row, mask, cot, load_sems,
     adj, adj_t, cm, cm_low, cm_high, gath, gath_t, masks, csend, crecv, acc, ysend, yrecv,
     near_send, near_recv, keep, keep_near, next_send, next_recv, zsend, zrecv,
-    starts, steps, part, a1s, a1r, half, a2s, a2r, a3r, a4r, wbuf, scale_col,
+    starts, steps, part, a1r, half, a2s, a2r, a3r, a4r, wbuf, scale_col,
     send_sems, recv_sems,
 ):
     sec = lax.axis_index("section")
@@ -209,8 +209,6 @@
 
         make(8 + n * 2 + h, NX + h, adj_t, n * 512, lanes, coefs_of)
 
-    prepare_block_t()
-
     for one in loads[:3]:
         one.wait()
     row = scale_row[...].astype(F32)
@@ -234,21 +232,18 @@
         state = {"z": {}, "one": {}, "two": {}, "opp": [], "y_t": {}, "core_t": []}
         for k in range(1, NZ):
             e = (NZ - OFFSET[k]) % NZ
-            run = pl.ds(k * ROWS, ROWS)
-            state["z"][k] = copy(own, gath.at[p, 0, run], z_peer(e))
-            state["y_t"][k] = copy(own_t, gath_t.at[p, 0, run], y_peer(e))
+            state["z"][k] = copy(own, gath.at[p, 0, pl.ds(k * ROWS, ROWS)], z_peer(e))
+            far = NY - k
+            e = (NY - OFFSET[far]) % NY
+            state["y_t"][far] = copy(own_t, gath_t.at[p, 0, pl.ds(far * ROWS, ROWS)], y_peer(e))
             if k == 2:
                 forward(p, 0, state)
-                forward_t(p, 0, state)
         return state
 
-    def forward_t(p, g, state):
-        lo, hi = GROUPS[g]
-        for k in range(lo, hi):
-            if k:
-                state["y_t"][k].wait_recv()
-        run = pl.ds(lo * ROWS, (hi - lo) * ROWS)
-        state["core_t"].append(copy(gath_t.at[p, 0, run], gath_t.at[p, 1, run], sibling))
+    def forward_t(p, state):
+        for k in range(NY - 1, 0, -1):
+            state["y_t"][k].wait_recv()
+        state["core_t"].append(copy(gath_t.at[p, 0], gath_t.at[p, 1], sibling))
 
     def forward(p, g, state):
         lo, hi = GROUPS[g]
@@ -357,39 +352,37 @@
 
     mask_copies = [copy(masks.at[z], masks.at[z], z_peer(e)) for e in range(1, NZ)]
     state = start_pass(0)
+    prepare_block_t()
     prepare_block()
     for one in mask_copies:
         one.wait_recv()
-    forward(0, 1, state)
-    forward_t(0, 1, state)
-    relay(0, 0, state)
     mask_columns_t()
     make_block_t(3, 0)
+    relay(0, 0, state)
     make_block_t(3, 1)
-    forward(0, 2, state)
-    forward_t(0, 2, state)
-    relay(0, 1, state)
+    forward(0, 1, state)
     make_block_t(1, 0)
     make_block_t(1, 1)
+    forward_t(0, state)
+    forward(0, 2, state)
+    relay(0, 1, state)
     make_block_t(2, 0)
-    forward(0, 3, state)
-    forward_t(0, 3, state)
-    relay(0, 2, state)
     make_block_t(2, 1)
     mask_columns()
-    for n in range(3):
-        make_block(n, 0)
+    make_block(0, 0)
     near_first(0, state)
-    relay(0, 3, state)
+    relay(0, 2, state)
     near_second(0)
+    make_block(1, 0)
+    make_block(2, 0)
     make_block(3, 0)
     make_block_t(0, 0)
     make_block_t(0, 1)
     make_block(0, 1)
-    make_block(1, 1)
     next_first(0, state)
     finish_gather(state)
     sums_first(0, state)
+    make_block(1, 1)
     make_block(2, 1)
     make_block(3, 1)
     product(0, 1)
@@ -414,31 +407,28 @@
     gath_t[1, 0, 0:ROWS] = error[:, HALF:]
 
     state = start_pass(1)
+    dims = (((0,), (0,)), ((), ()))
     part[...] = lax.dot_general(
-        sums_high, error, (((0,), (0,)), ((), ())), preferred_element_type=F32
-    )
+        sums_high, error, dims, preferred_element_type=F32
+    ) + lax.dot_general(sums_low, error, dims, preferred_element_type=F32)
     theirs = pl.multiple_of((1 - c) * 128, 128)
     mine = pl.multiple_of(c * 128, 128)
-    a1s[...] = part[pl.ds(theirs, 128), :].astype(BF16)
-    first = copy(a1s, a1r, sibling)
+    first = copy(part.at[pl.ds(theirs, 128)], a1r, sibling)
+    relay(1, 0, state)
     forward(1, 1, state)
-    forward_t(1, 1, state)
-    relay(1, 0, state)
 
     first.wait_recv()
-    half[...] = part[pl.ds(mine, 128), :] + a1r[...].astype(F32)
+    half[...] = part[pl.ds(mine, 128), :] + a1r[...]
     a2s[...] = half[...].astype(BF16)
     second = []
     for e in range(1, NY):
         at = pl.multiple_of(((y + e) % NY) * 16, 16)
         second.append(copy(a2s.at[pl.ds(at, 16)], a2r.at[e], y_peer(e)))
 
+    forward_t(1, state)
     forward(1, 2, state)
-    forward_t(1, 2, state)
     relay(1, 1, state)
-    forward(1, 3, state)
-    forward_t(1, 3, state)
-    relay(1, 2, state)
+    near_first(1, state)
 
     piece = half[pl.ds(pl.multiple_of(y * 16, 16), 16), :]
     for e in range(1, NY):
@@ -447,8 +437,7 @@
     a3r[z] = piece.astype(BF16)
     third = [copy(a3r.at[z], a3r.at[z], z_peer(e)) for e in range(1, NZ)]
 
-    near_first(1, state)
-    relay(1, 3, state)
+    relay(1, 2, state)
     near_second(1)
 
     for one in third:
@@ -538,8 +527,7 @@
             pltpu.VMEM((16, 16, 512), F32),
             pltpu.VMEM((NX + 2, 2, 8, 512), F32),
             pltpu.VMEM((256, 256), F32),
-            pltpu.VMEM((128, 256), BF16),
-            pltpu.VMEM((128, 256), BF16),
+            pltpu.VMEM((128, 256), F32),
             pltpu.VMEM((128, 256), F32),
             pltpu.VMEM((128, 256), BF16),
             pltpu.VMEM((NY, 16, 256), BF16),

time: 71.7 us -> 70.8 us (0.987)
  Pallas kernels: 70.9 us -> 70 us
    pallas_call x1, Pallas kernels: 70.2 us -> 69.3 us  [local(): pl.pallas_call(functools.partial(kernel, coef), out_shape=tuple((pltpu.VM...]
where the time goes in v2:
time: 70.8 us; the launch traced here: 70.7 us
  Pallas kernels  70 us (99%)
    pallas_call x1, Pallas kernels, local(): pl.pallas_call(functools.partial(kernel, coef), out_shape=tuple((pltpu.VM...  69.3 us

profile of v2, /device:TPU:1, one launch (start us, length us, event | category | flops | bytes accessed | tf_op | source)
XLA Modules:
  0.0 70.7 jit_solution(8541932502007791064)
XLA Ops:
  0.6 69.3 %shard_map.76 = (bf16[64,256]{1,0:T(8,128)(2,1)S(1)}, bf16[64,256]{1,0:T(8,128)(2,1)S(1)}, f32[256,256]{1,0:T(8,128)S(1)}) custom-call(bf16[64,256]{1,0:T(8,128)(2,1)} %feats_hbm.1, bf16[256,256]{1,0:T(8,128)(2,1)} %weight_hbm.1, bf16[1,64]{1,0:T(2,128)(2,1)} %bitcast.1, s32[2,256]{1,0:T(2,128)} %mask_hbm.1, bf16[64,256]{1,0:T(8,128)(2,1)} %cot_hbm.1), custom_call_target="tpu_custom_call" | custom-call | tf_op jit(solution)/shard_map/pallas_call | solution.py:494
  69.9 0.8 %shard_map.77 = (bf16[64,256]{1,0:T(8,128)(2,1)}, bf16[64,256]{1,0:T(8,128)(2,1)}, f32[256,256]{1,0:T(8,128)}) custom-call(bf16[64,256]{1,0:T(8,128)(2,1)S(1)} %get-tuple-element.6.refs_0_, bf16[64,256]{1,0:T(8,128)(2,1)S(1)} %get-tuple-element.7.refs_1_, f32[256,256]{1,0:T(8,128)S(1)} %get-tuple-element.8.refs_2_), custom_call_target="tpu_custom_call" | custom-call | tf_op jit(solution)/shard_map/pallas_call | solution.py:545

commit v3 on v2

--- a/solution.py
+++ b/solution.py
@@ -44,7 +44,7 @@
     feats_hbm, weight_hbm, scale_hbm, mask_hbm, cot_hbm,
     layer_out, grad_feats, grad_weight,
     feats, weight, scale_row, mask, cot, load_sems,
-    adj, adj_t, cm, cm_low, cm_high, gath, gath_t, masks, csend, crecv, acc, ysend, yrecv,
+    adj, cm, gath, gath_t, masks, csend, crecv, acc, ysend, yrecv,
     near_send, near_recv, keep, keep_near, next_send, next_recv, zsend, zrecv,
     starts, steps, part, a1r, half, a2s, a2r, a3r, a4r, wbuf, scale_col,
     send_sems, recv_sems,
@@ -133,25 +133,8 @@
             )
             cm[:, n * 512:(n + 1) * 512] = jnp.where(chosen > 0.5, coef, 0.0)
 
-    def mask_columns_t():
-        every = masks[...].reshape(64, HALF)
-        entry = lax.broadcasted_iota(jnp.int32, (HALF, 512), 0)
-        slot = lax.broadcasted_iota(jnp.int32, (HALF, 512), 1) >> 6
-        off = jnp.where((slot & 1) == 1, (slot + 1) >> 1, (8 - (slot >> 1)) & 7)
-        for h in range(2):
-            core_of = c if h == 0 else 1 - c
-            tile = ((z * NY + ((y + off) & 7)) * 2 + core_of) * 2 + x // 2
-            low = jnp.dot(every, (tile == entry).astype(F32), preferred_element_type=F32)
-            high = jnp.dot(every, (tile == entry + HALF).astype(F32), preferred_element_type=F32)
-            cm_low[:, h * 512:(h + 1) * 512] = jnp.where(low > 0.5, coef, 0.0)
-            cm_high[:, h * 512:(h + 1) * 512] = jnp.where(high > 0.5, coef, 0.0)
-
     def column_ids(n):
         return ((((z + col_off) & 7) * NY + y) * 2 + c) * 256 + columns_x[n] * ROWS + (col_j & 63)
-
-    def column_ids_t(h):
-        core_of = c if h == 0 else 1 - c
-        return ((z * NY + ((y + col_off) & 7)) * 2 + core_of) * 256 + x * ROWS + (col_j & 63)
 
     def prepare(unit, a, b):
         first = fold(fold(a * b))
@@ -171,43 +154,25 @@
                 a = ((z * NY) * 2 + side_core(side)) * 256 + x * ROWS + row_i
                 prepare(n * 2 + side, a, b)
 
-    def prepare_block_t():
-        for h in range(2):
-            b = column_ids_t(h)
-            prepare_steps(NX + h, b, 4096)
-            for n in range(NX):
-                a = (y * 2 + c) * 256 + columns_x[n] * ROWS + row_i
-                prepare(8 + n * 2 + h, a, b)
-
-    def make(unit, number, target, top, lanes, coefs_of):
-        step16 = jnp.concatenate([steps[number, 0]] * 2, axis=0)
-        leap = jnp.concatenate([steps[number, 1]] * 2, axis=0)
-
-        def run(turn, u0):
-            coefs = coefs_of(turn)
+    def make_block(n, side):
+        lanes = slice(n * 512, (n + 1) * 512)
+        step16 = jnp.concatenate([steps[n, 0]] * 2, axis=0)
+        leap = jnp.concatenate([steps[n, 1]] * 2, axis=0)
+
+        def run(yy, u0):
+            off = (yy - y + NY) % NY
+            late = off // 5
+            slot = (off + 7) // 8 * ((1 - late) * (2 * off - 1) + late * (16 - 2 * off))
+            coefs = cm[pl.ds(side * 8 + yy, 1), lanes]
             u = u0
             for s in range(4):
-                at = pl.multiple_of(top + turn * ROWS + s * 16, 16)
-                target[pl.ds(at, 16), lanes] = (u * coefs).astype(BF16)
+                at = pl.multiple_of(side * 512 + slot * ROWS + s * 16, 16)
+                adj[pl.ds(at, 16), lanes] = (u * coefs).astype(BF16)
                 if s < 3:
                     u = add_wrapped(u, step16)
             return add_wrapped(u0, leap)
 
-        lax.fori_loop(0, 8, run, starts[unit])
-
-    def make_block(n, side):
-        lanes = slice(n * 512, (n + 1) * 512)
-        make(n * 2 + side, n, adj, side * 512, lanes, lambda yy: cm[pl.ds(side * 8 + yy, 1), lanes])
-
-    def make_block_t(n, h):
-        lanes = slice(h * 512, (h + 1) * 512)
-        tile = columns_x[n] // 2
-
-        def coefs_of(zz):
-            low = cm_low[pl.ds(zz * 8 + tile, 1), lanes]
-            return low + cm_high[pl.ds(zz * 8 + tile + 2, 1), lanes]
-
-        make(8 + n * 2 + h, NX + h, adj_t, n * 512, lanes, coefs_of)
+        lax.fori_loop(0, 8, run, starts[n * 2 + side])
 
     for one in loads[:3]:
         one.wait()
@@ -287,19 +252,24 @@
         ysend[p] = total.astype(BF16)
         state["y"] = {}
         for e in (4, 3, 5, 2, 6, 1, 7):
-            at = pl.multiple_of(((y + e) % NY) * ROWS, ROWS)
-            state["y"][e] = copy(ysend.at[p, pl.ds(at, ROWS)], yrecv.at[p, e], y_peer(e))
+            run = pl.ds(SLOT[e] * ROWS, ROWS)
+            state["y"][e] = copy(ysend.at[p, run], yrecv.at[p, e], y_peer(e))
 
     def sums_last(p, state):
-        total = acc[pl.ds(pl.multiple_of(y * ROWS, ROWS), ROWS), :]
+        total = acc[0:ROWS]
         for e in (1, 7, 2, 6, 3, 5, 4):
             state["y"][e].wait_recv()
             total = total + yrecv[p, e].astype(F32)
         return total
 
     def product_t(p, lo, hi):
-        right = gath_t[p].reshape(2 * NY * ROWS, HALF)
-        return jnp.dot(adj_t[lo:hi, :], right, preferred_element_type=F32)
+        dims = (((0,), (0,)), ((), ()))
+        turned = lax.dot_general(
+            gath_t[p, 1], adj[0:512, lo:hi], dims, preferred_element_type=F32
+        ) + lax.dot_general(
+            gath_t[p, 0], adj[512:1024, lo:hi], dims, preferred_element_type=F32
+        )
+        return turned.T
 
     def near_first(p, state):
         for one in state["core_t"]:
@@ -340,11 +310,11 @@
         zsend[p] = total.astype(BF16)
         state["z_t"] = {}
         for e in (4, 3, 5, 2, 6, 1, 7):
-            at = pl.multiple_of(((z + e) % NZ) * ROWS, ROWS)
-            state["z_t"][e] = copy(zsend.at[p, pl.ds(at, ROWS)], zrecv.at[p, e], z_peer(e))
+            run = pl.ds(SLOT[e] * ROWS, ROWS)
+            state["z_t"][e] = copy(zsend.at[p, run], zrecv.at[p, e], z_peer(e))
 
     def sums_last_t(p, state):
-        total = keep[pl.ds(pl.multiple_of(z * ROWS, ROWS), ROWS), :]
+        total = keep[0:ROWS]
         for e in (1, 7, 2, 6, 3, 5, 4):
             state["z_t"][e].wait_recv()
             total = total + zrecv[p, e].astype(F32)
@@ -352,42 +322,32 @@
 
     mask_copies = [copy(masks.at[z], masks.at[z], z_peer(e)) for e in range(1, NZ)]
     state = start_pass(0)
-    prepare_block_t()
     prepare_block()
     for one in mask_copies:
         one.wait_recv()
-    mask_columns_t()
-    make_block_t(3, 0)
+    mask_columns()
+    make_block(3, 0)
     relay(0, 0, state)
-    make_block_t(3, 1)
+    make_block(3, 1)
     forward(0, 1, state)
-    make_block_t(1, 0)
-    make_block_t(1, 1)
+    make_block(1, 0)
+    make_block(1, 1)
     forward_t(0, state)
     forward(0, 2, state)
     relay(0, 1, state)
-    make_block_t(2, 0)
-    make_block_t(2, 1)
-    mask_columns()
-    make_block(0, 0)
+    make_block(2, 0)
+    make_block(2, 1)
     near_first(0, state)
     relay(0, 2, state)
     near_second(0)
-    make_block(1, 0)
-    make_block(2, 0)
-    make_block(3, 0)
-    make_block_t(0, 0)
-    make_block_t(0, 1)
+    make_block(0, 0)
     make_block(0, 1)
     next_first(0, state)
     finish_gather(state)
     sums_first(0, state)
-    make_block(1, 1)
-    make_block(2, 1)
-    make_block(3, 1)
     product(0, 1)
+    next_second(0, state)
     sums_second(0, state)
-    next_second(0, state)
     sums = jnp.concatenate([sums_last(0, state), sums_last_t(0, state)], axis=1)
 
     for one in loads[3:]:
@@ -406,6 +366,8 @@
     gath[1, 0, 0:ROWS] = error[:, :HALF]
     gath_t[1, 0, 0:ROWS] = error[:, HALF:]
 
+    earlier = list(started)
+
     state = start_pass(1)
     dims = (((0,), (0,)), ((), ()))
     part[...] = lax.dot_general(
@@ -414,6 +376,8 @@
     theirs = pl.multiple_of((1 - c) * 128, 128)
     mine = pl.multiple_of(c * 128, 128)
     first = copy(part.at[pl.ds(theirs, 128)], a1r, sibling)
+    for one in earlier:
+        one.wait_send()
     relay(1, 0, state)
     forward(1, 1, state)
 
@@ -472,7 +436,7 @@
     ).astype(BF16)
     sixth.wait_recv()
     grad_weight[...] = wbuf[...].astype(F32)
-    for one in started:
+    for one in started[len(earlier):]:
         one.wait_send()
 
 
@@ -504,10 +468,7 @@
             pltpu.VMEM((ROWS, hidden), BF16),
             pltpu.SemaphoreType.DMA((5,)),
             pltpu.VMEM((1024, 2048), BF16),
-            pltpu.VMEM((2048, 1024), BF16),
             pltpu.VMEM((16, 2048), F32),
-            pltpu.VMEM((64, 1024), F32),
-            pltpu.VMEM((64, 1024), F32),
             pltpu.VMEM((2, NX, NZ * ROWS, HALF), BF16),
             pltpu.VMEM((2, 2, NY * ROWS, HALF), BF16),
             pltpu.VMEM((NZ, 8, HALF), F32),
@@ -524,8 +485,8 @@
             pltpu.VMEM((2, 2, 256, HALF), BF16),
             pltpu.VMEM((2, 512, HALF), BF16),
             pltpu.VMEM((2, NZ, ROWS, HALF), BF16),
-            pltpu.VMEM((16, 16, 512), F32),
-            pltpu.VMEM((NX + 2, 2, 8, 512), F32),
+            pltpu.VMEM((8, 16, 512), F32),
+            pltpu.VMEM((NX, 2, 8, 512), F32),
             pltpu.VMEM((256, 256), F32),
             pltpu.VMEM((128, 256), F32),
             pltpu.VMEM((128, 256), F32),

time: 70.8 us -> 69.6 us (0.983)
  Pallas kernels: 70 us -> 68.8 us
    pallas_call x1, Pallas kernels: 69.3 us -> 68.1 us  [local(): pl.pallas_call(functools.partial(kernel, coef), out_shape=tuple((pltpu.VM...]
where the time goes in v3:
time: 69.6 us; the launch traced here: 69.5 us
  Pallas kernels  68.8 us (99%)
    pallas_call x1, Pallas kernels, local(): pl.pallas_call(functools.partial(kernel, coef), out_shape=tuple((pltpu.VM...  68.1 us

profile of v3, /device:TPU:1, one launch (start us, length us, event | category | flops | bytes accessed | tf_op | source)
XLA Modules:
  0.0 69.5 jit_solution(3448789543308416860)
XLA Ops:
  0.6 68.1 %shard_map.76 = (bf16[64,256]{1,0:T(8,128)(2,1)S(1)}, bf16[64,256]{1,0:T(8,128)(2,1)S(1)}, f32[256,256]{1,0:T(8,128)S(1)}) custom-call(bf16[64,256]{1,0:T(8,128)(2,1)} %feats_hbm.1, bf16[256,256]{1,0:T(8,128)(2,1)} %weight_hbm.1, bf16[1,64]{1,0:T(2,128)(2,1)} %bitcast.1, s32[2,256]{1,0:T(2,128)} %mask_hbm.1, bf16[64,256]{1,0:T(8,128)(2,1)} %cot_hbm.1), custom_call_target="tpu_custom_call" | custom-call | tf_op jit(solution)/shard_map/pallas_call | solution.py:458
  68.7 0.8 %shard_map.77 = (bf16[64,256]{1,0:T(8,128)(2,1)}, bf16[64,256]{1,0:T(8,128)(2,1)}, f32[256,256]{1,0:T(8,128)}) custom-call(bf16[64,256]{1,0:T(8,128)(2,1)S(1)} %get-tuple-element.6.refs_0_, bf16[64,256]{1,0:T(8,128)(2,1)S(1)} %get-tuple-element.7.refs_1_, f32[256,256]{1,0:T(8,128)S(1)} %get-tuple-element.8.refs_2_), custom_call_target="tpu_custom_call" | custom-call | tf_op jit(solution)/shard_map/pallas_call | solution.py:506

commit v4 on v3

--- a/solution.py
+++ b/solution.py
@@ -17,7 +17,7 @@
 OFFSET = (0, 1, 7, 2, 6, 3, 5, 4)
 SLOT = {off: k for k, off in enumerate(OFFSET)}
 GROUPS = ((0, 1), (1, 5), (5, 8))
-COPIES = 160
+COPIES = 80
 BF16 = jnp.bfloat16
 F32 = jnp.float32
 
@@ -90,15 +90,30 @@
         pl.semaphore_signal(barrier, inc=1, device_id=peer, device_id_type=MESH)
 
     started = []
+    numbers = iter(range(COPIES))
+
+    class Batch:
+        def __init__(self, view, target):
+            number = next(numbers)
+            self.send_sem, self.recv_sem = send_sems.at[number], recv_sems.at[number]
+            self.whole = self.describe(view, view, target)
+            started.append(self.whole)
+
+        def describe(self, src, dst, target):
+            return pltpu.make_async_remote_copy(
+                src_ref=src, dst_ref=dst, send_sem=self.send_sem, recv_sem=self.recv_sem,
+                device_id=target, device_id_type=MESH,
+            )
+
+        def start(self, src, dst, target):
+            self.describe(src, dst, target).start()
+
+        def wait_recv(self):
+            self.whole.wait_recv()
 
     def copy(src, dst, target):
-        number = len(started)
-        one = pltpu.make_async_remote_copy(
-            src_ref=src, dst_ref=dst, send_sem=send_sems.at[number],
-            recv_sem=recv_sems.at[number], device_id=target, device_id_type=MESH,
-        )
-        one.start()
-        started.append(one)
+        one = Batch(dst, target)
+        one.start(src, dst, target)
         return one
 
     col_j = lax.broadcasted_iota(jnp.int32, (16, 512), 1)
@@ -195,26 +210,28 @@
         own = gath.at[p, 0, pl.ds(0, ROWS)]
         own_t = gath_t.at[p, 0, pl.ds(0, ROWS)]
         state = {"z": {}, "one": {}, "two": {}, "opp": [], "y_t": {}, "core_t": []}
+        for g, (lo, hi) in enumerate(GROUPS[1:], 1):
+            state["z"][g] = Batch(gath.at[p, 0, pl.ds(lo * ROWS, (hi - lo) * ROWS)], z_peer(1))
+        state["y_t"] = Batch(gath_t.at[p, 0, pl.ds(ROWS, (NY - 1) * ROWS)], y_peer(1))
         for k in range(1, NZ):
             e = (NZ - OFFSET[k]) % NZ
-            state["z"][k] = copy(own, gath.at[p, 0, pl.ds(k * ROWS, ROWS)], z_peer(e))
+            g = 1 if k < GROUPS[1][1] else 2
+            state["z"][g].start(own, gath.at[p, 0, pl.ds(k * ROWS, ROWS)], z_peer(e))
             far = NY - k
             e = (NY - OFFSET[far]) % NY
-            state["y_t"][far] = copy(own_t, gath_t.at[p, 0, pl.ds(far * ROWS, ROWS)], y_peer(e))
+            state["y_t"].start(own_t, gath_t.at[p, 0, pl.ds(far * ROWS, ROWS)], y_peer(e))
             if k == 2:
                 forward(p, 0, state)
         return state
 
     def forward_t(p, state):
-        for k in range(NY - 1, 0, -1):
-            state["y_t"][k].wait_recv()
+        state["y_t"].wait_recv()
         state["core_t"].append(copy(gath_t.at[p, 0], gath_t.at[p, 1], sibling))
 
     def forward(p, g, state):
         lo, hi = GROUPS[g]
-        for k in range(lo, hi):
-            if k:
-                state["z"][k].wait_recv()
+        if g:
+            state["z"][g].wait_recv()
         run = pl.ds(lo * ROWS, (hi - lo) * ROWS)
         state["one"][g] = copy(gath.at[p, 0, run], gath.at[p, 1, run], east)
         state["two"][g] = copy(gath.at[p, 0, run], gath.at[p, 2, run], west)
@@ -250,15 +267,15 @@
         total = acc[...] + crecv[p].astype(F32)
         acc[...] = total
         ysend[p] = total.astype(BF16)
-        state["y"] = {}
+        state["y"] = Batch(yrecv.at[p, pl.ds(1, NY - 1)], y_peer(1))
         for e in (4, 3, 5, 2, 6, 1, 7):
             run = pl.ds(SLOT[e] * ROWS, ROWS)
-            state["y"][e] = copy(ysend.at[p, run], yrecv.at[p, e], y_peer(e))
+            state["y"].start(ysend.at[p, run], yrecv.at[p, e], y_peer(e))
 
     def sums_last(p, state):
         total = acc[0:ROWS]
-        for e in (1, 7, 2, 6, 3, 5, 4):
-            state["y"][e].wait_recv()
+        state["y"].wait_recv()
+        for e in range(1, NY):
             total = total + yrecv[p, e].astype(F32)
         return total
 
@@ -308,23 +325,24 @@
         total = keep[...] + next_recv[p].reshape(512, HALF).astype(F32)
         keep[...] = total
         zsend[p] = total.astype(BF16)
-        state["z_t"] = {}
+        state["z_t"] = Batch(zrecv.at[p, pl.ds(1, NZ - 1)], z_peer(1))
         for e in (4, 3, 5, 2, 6, 1, 7):
             run = pl.ds(SLOT[e] * ROWS, ROWS)
-            state["z_t"][e] = copy(zsend.at[p, run], zrecv.at[p, e], z_peer(e))
+            state["z_t"].start(zsend.at[p, run], zrecv.at[p, e], z_peer(e))
 
     def sums_last_t(p, state):
         total = keep[0:ROWS]
-        for e in (1, 7, 2, 6, 3, 5, 4):
-            state["z_t"][e].wait_recv()
+        state["z_t"].wait_recv()
+        for e in range(1, NZ):
             total = total + zrecv[p, e].astype(F32)
         return total
 
-    mask_copies = [copy(masks.at[z], masks.at[z], z_peer(e)) for e in range(1, NZ)]
+    mask_copies = Batch(masks.at[pl.ds(0, NZ - 1)], z_peer(1))
+    for e in range(1, NZ):
+        mask_copies.start(masks.at[z], masks.at[z], z_peer(e))
     state = start_pass(0)
     prepare_block()
-    for one in mask_copies:
-        one.wait_recv()
+    mask_copies.wait_recv()
     mask_columns()
     make_block(3, 0)
     relay(0, 0, state)
@@ -384,10 +402,10 @@
     first.wait_recv()
     half[...] = part[pl.ds(mine, 128), :] + a1r[...]
     a2s[...] = half[...].astype(BF16)
-    second = []
+    second = Batch(a2r.at[pl.ds(1, NY - 1)], y_peer(1))
     for e in range(1, NY):
         at = pl.multiple_of(((y + e) % NY) * 16, 16)
-        second.append(copy(a2s.at[pl.ds(at, 16)], a2r.at[e], y_peer(e)))
+        second.start(a2s.at[pl.ds(at, 16)], a2r.at[e], y_peer(e))
 
     forward_t(1, state)
     forward(1, 2, state)
@@ -395,39 +413,42 @@
     near_first(1, state)
 
     piece = half[pl.ds(pl.multiple_of(y * 16, 16), 16), :]
+    second.wait_recv()
     for e in range(1, NY):
-        second[e - 1].wait_recv()
         piece = piece + a2r[e].astype(F32)
     a3r[z] = piece.astype(BF16)
-    third = [copy(a3r.at[z], a3r.at[z], z_peer(e)) for e in range(1, NZ)]
+    third = Batch(a3r.at[pl.ds(0, NZ - 1)], z_peer(1))
+    for e in range(1, NZ):
+        third.start(a3r.at[z], a3r.at[z], z_peer(e))
 
     relay(1, 2, state)
     near_second(1)
 
-    for one in third:
-        one.wait_recv()
+    third.wait_recv()
     piece = a3r[0].astype(F32)
     for n in range(1, NZ):
         piece = piece + a3r[n].astype(F32)
     a4r[x] = piece
-    fourth = [copy(a4r.at[x], a4r.at[x], x_peer(e)) for e in range(1, NX)]
+    fourth = Batch(a4r.at[pl.ds(0, NX - 1)], x_peer(1))
+    for e in range(1, NX):
+        fourth.start(a4r.at[x], a4r.at[x], x_peer(e))
 
     next_first(1, state)
     finish_gather(state)
     sums_first(1, state)
     product(1, 1)
 
-    for one in fourth:
-        one.wait_recv()
+    fourth.wait_recv()
     piece = (a4r[0] + a4r[1]) + (a4r[2] + a4r[3])
     at = pl.multiple_of(c * 128 + y * 16, 16)
     wbuf[pl.ds(at, 16), :] = piece.astype(BF16)
-    fifth = [copy(wbuf.at[pl.ds(at, 16)], wbuf.at[pl.ds(at, 16)], y_peer(e)) for e in range(1, NY)]
+    fifth = Batch(wbuf.at[pl.ds(0, 16 * (NY - 1))], y_peer(1))
+    for e in range(1, NY):
+        fifth.start(wbuf.at[pl.ds(at, 16)], wbuf.at[pl.ds(at, 16)], y_peer(e))
 
     sums_second(1, state)
     next_second(1, state)
-    for one in fifth:
-        one.wait_recv()
+    fifth.wait_recv()
     sixth = copy(wbuf.at[pl.ds(mine, 128)], wbuf.at[pl.ds(mine, 128)], sibling)
     back = jnp.concatenate([sums_last(1, state), sums_last_t(1, state)], axis=1)
     vgrad = (scale * back).astype(BF16)

time: 69.6 us -> 68.3 us (0.981)
  Pallas kernels: 68.8 us -> 67.6 us
    pallas_call x1, Pallas kernels: 68.1 us -> 66.8 us  [local(): pl.pallas_call(functools.partial(kernel, coef), out_shape=tuple((pltpu.VM...]
where the time goes in v4:
time: 68.3 us; the launch traced here: 68.2 us
  Pallas kernels  67.6 us (99%)
    pallas_call x1, Pallas kernels, local(): pl.pallas_call(functools.partial(kernel, coef), out_shape=tuple((pltpu.VM...  66.8 us

profile of v4, /device:TPU:1, one launch (start us, length us, event | category | flops | bytes accessed | tf_op | source)
XLA Modules:
  0.0 68.2 jit_solution(11155648425666612991)
XLA Ops:
  0.6 66.8 %shard_map.76 = (bf16[64,256]{1,0:T(8,128)(2,1)S(1)}, bf16[64,256]{1,0:T(8,128)(2,1)S(1)}, f32[256,256]{1,0:T(8,128)S(1)}) custom-call(bf16[64,256]{1,0:T(8,128)(2,1)} %feats_hbm.1, bf16[256,256]{1,0:T(8,128)(2,1)} %weight_hbm.1, bf16[1,64]{1,0:T(2,128)(2,1)} %bitcast.1, s32[2,256]{1,0:T(2,128)} %mask_hbm.1, bf16[64,256]{1,0:T(8,128)(2,1)} %cot_hbm.1), custom_call_target="tpu_custom_call" | custom-call | tf_op jit(solution)/shard_map/pallas_call | solution.py:479
  67.5 0.8 %shard_map.77 = (bf16[64,256]{1,0:T(8,128)(2,1)}, bf16[64,256]{1,0:T(8,128)(2,1)}, f32[256,256]{1,0:T(8,128)}) custom-call(bf16[64,256]{1,0:T(8,128)(2,1)S(1)} %get-tuple-element.6.refs_0_, bf16[64,256]{1,0:T(8,128)(2,1)S(1)} %get-tuple-element.7.refs_1_, f32[256,256]{1,0:T(8,128)S(1)} %get-tuple-element.8.refs_2_), custom_call_target="tpu_custom_call" | custom-call | tf_op jit(solution)/shard_map/pallas_call | solution.py:527

commit v5 on v4

--- a/solution.py
+++ b/solution.py
@@ -313,6 +313,8 @@
         state["far_w"].wait_recv()
         next_send[p, 1] = (keep_near[1] + near_recv[p, 1, 256:512].astype(F32)).astype(BF16)
         state["next_e"] = copy(next_send.at[p, 1], next_recv.at[p, 1], east)
+
+    def next_own(p, state):
         value = product_t(p, 0, 512)
         state["near_e"].wait_recv()
         state["near_w"].wait_recv()
@@ -320,15 +322,16 @@
         keep[256:512] = value[256:] + near_recv[p, 1, 0:256].astype(F32)
 
     def next_second(p, state):
-        state["next_w"].wait_recv()
-        state["next_e"].wait_recv()
-        total = keep[...] + next_recv[p].reshape(512, HALF).astype(F32)
-        keep[...] = total
-        zsend[p] = total.astype(BF16)
         state["z_t"] = Batch(zrecv.at[p, pl.ds(1, NZ - 1)], z_peer(1))
-        for e in (4, 3, 5, 2, 6, 1, 7):
-            run = pl.ds(SLOT[e] * ROWS, ROWS)
-            state["z_t"].start(zsend.at[p, run], zrecv.at[p, e], z_peer(e))
+        for part_at, arrival, offsets in ((1, "next_e", (4, 3, 5, 6)), (0, "next_w", (2, 1, 7))):
+            state[arrival].wait_recv()
+            rows = slice(part_at * 256, (part_at + 1) * 256)
+            total = keep[rows] + next_recv[p, part_at].astype(F32)
+            zsend[p, rows] = total.astype(BF16)
+            for e in offsets:
+                run = pl.ds(SLOT[e] * ROWS, ROWS)
+                state["z_t"].start(zsend.at[p, run], zrecv.at[p, e], z_peer(e))
+        keep[0:ROWS] = total[0:ROWS]
 
     def sums_last_t(p, state):
         total = keep[0:ROWS]
@@ -363,6 +366,7 @@
     next_first(0, state)
     finish_gather(state)
     sums_first(0, state)
+    next_own(0, state)
     product(0, 1)
     next_second(0, state)
     sums_second(0, state)
@@ -423,6 +427,9 @@
 
     relay(1, 2, state)
     near_second(1)
+    next_first(1, state)
+    finish_gather(state)
+    sums_first(1, state)
 
     third.wait_recv()
     piece = a3r[0].astype(F32)
@@ -433,10 +440,9 @@
     for e in range(1, NX):
         fourth.start(a4r.at[x], a4r.at[x], x_peer(e))
 
-    next_first(1, state)
-    finish_gather(state)
-    sums_first(1, state)
+    next_own(1, state)
     product(1, 1)
+    next_second(1, state)
 
     fourth.wait_recv()
     piece = (a4r[0] + a4r[1]) + (a4r[2] + a4r[3])
@@ -445,9 +451,7 @@
     fifth = Batch(wbuf.at[pl.ds(0, 16 * (NY - 1))], y_peer(1))
     for e in range(1, NY):
         fifth.start(wbuf.at[pl.ds(at, 16)], wbuf.at[pl.ds(at, 16)], y_peer(e))
-
     sums_second(1, state)
-    next_second(1, state)
     fifth.wait_recv()
     sixth = copy(wbuf.at[pl.ds(mine, 128)], wbuf.at[pl.ds(mine, 128)], sibling)
     back = jnp.concatenate([sums_last(1, state), sums_last_t(1, state)], axis=1)

time: 68.3 us -> 68 us (level)
  no operation moved by 1% of the time
where the time goes in v5:
time: 68 us; the launch traced here: 67.9 us
  Pallas kernels  67.3 us (99%)
    pallas_call x1, Pallas kernels, local(): pl.pallas_call(functools.partial(kernel, coef), out_shape=tuple((pltpu.VM...  66.5 us

profile of v5, /device:TPU:1, one launch (start us, length us, event | category | flops | bytes accessed | tf_op | source)
XLA Modules:
  0.0 67.9 jit_solution(17481879475687202131)
XLA Ops:
  0.6 66.5 %shard_map.76 = (bf16[64,256]{1,0:T(8,128)(2,1)S(1)}, bf16[64,256]{1,0:T(8,128)(2,1)S(1)}, f32[256,256]{1,0:T(8,128)S(1)}) custom-call(bf16[64,256]{1,0:T(8,128)(2,1)} %feats_hbm.1, bf16[256,256]{1,0:T(8,128)(2,1)} %weight_hbm.1, bf16[1,64]{1,0:T(2,128)(2,1)} %bitcast.1, s32[2,256]{1,0:T(2,128)} %mask_hbm.1, bf16[64,256]{1,0:T(8,128)(2,1)} %cot_hbm.1), custom_call_target="tpu_custom_call" | custom-call | tf_op jit(solution)/shard_map/pallas_call | solution.py:483
  67.1 0.8 %shard_map.77 = (bf16[64,256]{1,0:T(8,128)(2,1)}, bf16[64,256]{1,0:T(8,128)(2,1)}, f32[256,256]{1,0:T(8,128)}) custom-call(bf16[64,256]{1,0:T(8,128)(2,1)S(1)} %get-tuple-element.6.refs_0_, bf16[64,256]{1,0:T(8,128)(2,1)S(1)} %get-tuple-element.7.refs_1_, f32[256,256]{1,0:T(8,128)S(1)} %get-tuple-element.8.refs_2_), custom_call_target="tpu_custom_call" | custom-call | tf_op jit(solution)/shard_map/pallas_call | solution.py:531

commit v6 on v5

--- a/solution.py
+++ b/solution.py
@@ -211,27 +211,42 @@
         own_t = gath_t.at[p, 0, pl.ds(0, ROWS)]
         state = {"z": {}, "one": {}, "two": {}, "opp": [], "y_t": {}, "core_t": []}
         for g, (lo, hi) in enumerate(GROUPS[1:], 1):
-            state["z"][g] = Batch(gath.at[p, 0, pl.ds(lo * ROWS, (hi - lo) * ROWS)], z_peer(1))
-        state["y_t"] = Batch(gath_t.at[p, 0, pl.ds(ROWS, (NY - 1) * ROWS)], y_peer(1))
-        for k in range(1, NZ):
+            run = pl.ds(lo * ROWS, (hi - lo) * ROWS)
+            state["z"][g] = Batch(gath.at[p, 0, run], z_peer(1))
+            state["y_t"][g] = Batch(gath_t.at[p, 0, run], y_peer(1))
+        for k in range(1, 5):
             e = (NZ - OFFSET[k]) % NZ
-            g = 1 if k < GROUPS[1][1] else 2
-            state["z"][g].start(own, gath.at[p, 0, pl.ds(k * ROWS, ROWS)], z_peer(e))
-            far = NY - k
-            e = (NY - OFFSET[far]) % NY
-            state["y_t"].start(own_t, gath_t.at[p, 0, pl.ds(far * ROWS, ROWS)], y_peer(e))
+            run = pl.ds(k * ROWS, ROWS)
+            state["z"][1].start(own, gath.at[p, 0, run], z_peer(e))
+            state["y_t"][1].start(own_t, gath_t.at[p, 0, run], y_peer(e))
             if k == 2:
                 forward(p, 0, state)
         return state
 
+    def spread(blocks, batch, peer):
+        def rows(slot, lo, hi):
+            return blocks.at[pl.ds(slot * ROWS + lo, hi - lo)]
+
+        cut = ROWS // 2
+        batch.start(rows(3, 0, ROWS), rows(5, 0, ROWS), peer(7))
+        batch.start(rows(4, 0, ROWS), rows(6, 0, ROWS), peer(1))
+        batch.start(rows(3, 0, cut), rows(7, 0, cut), peer(6))
+        batch.start(rows(4, cut, ROWS), rows(7, cut, ROWS), peer(2))
+
+    def spread_t(p, state):
+        state["y_t"][1].wait_recv()
+        spread(gath_t.at[p, 0], state["y_t"][2], y_peer)
+
     def forward_t(p, state):
-        state["y_t"].wait_recv()
+        state["y_t"][2].wait_recv()
         state["core_t"].append(copy(gath_t.at[p, 0], gath_t.at[p, 1], sibling))
 
     def forward(p, g, state):
         lo, hi = GROUPS[g]
         if g:
             state["z"][g].wait_recv()
+        if g == 1:
+            spread(gath.at[p, 0], state["z"][2], z_peer)
         run = pl.ds(lo * ROWS, (hi - lo) * ROWS)
         state["one"][g] = copy(gath.at[p, 0, run], gath.at[p, 1, run], east)
         state["two"][g] = copy(gath.at[p, 0, run], gath.at[p, 2, run], west)
@@ -346,11 +361,12 @@
     state = start_pass(0)
     prepare_block()
     mask_copies.wait_recv()
+    forward(0, 1, state)
+    spread_t(0, state)
+    relay(0, 0, state)
     mask_columns()
     make_block(3, 0)
-    relay(0, 0, state)
     make_block(3, 1)
-    forward(0, 1, state)
     make_block(1, 0)
     make_block(1, 1)
     forward_t(0, state)
@@ -398,10 +414,11 @@
     theirs = pl.multiple_of((1 - c) * 128, 128)
     mine = pl.multiple_of(c * 128, 128)
     first = copy(part.at[pl.ds(theirs, 128)], a1r, sibling)
+    forward(1, 1, state)
+    spread_t(1, state)
+    relay(1, 0, state)
     for one in earlier:
         one.wait_send()
-    relay(1, 0, state)
-    forward(1, 1, state)
 
     first.wait_recv()
     half[...] = part[pl.ds(mine, 128), :] + a1r[...]

time: 68 us -> 69.6 us (1.024)
  Pallas kernels: 67.3 us -> 68.8 us
    pallas_call x1, Pallas kernels: 66.5 us -> 68 us  [local(): pl.pallas_call(functools.partial(kernel, coef), out_shape=tuple((pltpu.VM...]
where the time goes in v6:
time: 69.6 us; the launch traced here: 69.4 us
  Pallas kernels  68.8 us (99%)
    pallas_call x1, Pallas kernels, local(): pl.pallas_call(functools.partial(kernel, coef), out_shape=tuple((pltpu.VM...  68 us

profile of v6, /device:TPU:1, one launch (start us, length us, event | category | flops | bytes accessed | tf_op | source)
XLA Modules:
  0.0 69.4 jit_solution(6687819606366401824)
XLA Ops:
  0.6 68.0 %shard_map.76 = (bf16[64,256]{1,0:T(8,128)(2,1)S(1)}, bf16[64,256]{1,0:T(8,128)(2,1)S(1)}, f32[256,256]{1,0:T(8,128)S(1)}) custom-call(bf16[64,256]{1,0:T(8,128)(2,1)} %feats_hbm.1, bf16[256,256]{1,0:T(8,128)(2,1)} %weight_hbm.1, bf16[1,64]{1,0:T(2,128)(2,1)} %bitcast.1, s32[2,256]{1,0:T(2,128)} %mask_hbm.1, bf16[64,256]{1,0:T(8,128)(2,1)} %cot_hbm.1), custom_call_target="tpu_custom_call" | custom-call | tf_op jit(solution)/shard_map/pallas_call | solution.py:500
  68.7 0.8 %shard_map.77 = (bf16[64,256]{1,0:T(8,128)(2,1)}, bf16[64,256]{1,0:T(8,128)(2,1)}, f32[256,256]{1,0:T(8,128)}) custom-call(bf16[64,256]{1,0:T(8,128)(2,1)S(1)} %get-tuple-element.6.refs_0_, bf16[64,256]{1,0:T(8,128)(2,1)S(1)} %get-tuple-element.7.refs_1_, f32[256,256]{1,0:T(8,128)S(1)} %get-tuple-element.8.refs_2_), custom_call_target="tpu_custom_call" | custom-call | tf_op jit(solution)/shard_map/pallas_call | solution.py:548

commit v7 on v5

--- a/solution.py
+++ b/solution.py
@@ -18,6 +18,7 @@
 SLOT = {off: k for k, off in enumerate(OFFSET)}
 GROUPS = ((0, 1), (1, 5), (5, 8))
 COPIES = 80
+BOARD = tuple((d, e) for d in range(2) for e in range(NX) if d or e)
 BF16 = jnp.bfloat16
 F32 = jnp.float32
 
@@ -46,7 +47,7 @@
     feats, weight, scale_row, mask, cot, load_sems,
     adj, cm, gath, gath_t, masks, csend, crecv, acc, ysend, yrecv,
     near_send, near_recv, keep, keep_near, next_send, next_recv, zsend, zrecv,
-    starts, steps, part, a1r, half, a2s, a2r, a3r, a4r, wbuf, scale_col,
+    starts, steps, part, part_low, board_in, tiles, tiles_in, ring, whole, wbuf, scale_col,
     send_sems, recv_sems,
 ):
     sec = lax.axis_index("section")
@@ -70,8 +71,11 @@
     def y_peer(e):
         return device(z, (y + e) % NY, c, x)
 
-    def x_peer(e):
-        return device(z, y, c, (x + e) % NX)
+    def board_index(d, e):
+        return (c + d) % 2 * NX + (x + e) % NX
+
+    def board_peer(d, e):
+        return device(z, y, (c + d) % 2, (x + e) % NX)
 
     loads = [
         pltpu.make_async_copy(src, dst, load_sems.at[n])
@@ -85,7 +89,7 @@
 
     barrier = pltpu.get_barrier_semaphore()
     peers = [z_peer(e) for e in range(1, NZ)] + [y_peer(e) for e in range(1, NY)]
-    peers += [x_peer(e) for e in range(1, NX)] + [sibling]
+    peers += [board_peer(d, e) for d, e in BOARD]
     for peer in peers:
         pl.semaphore_signal(barrier, inc=1, device_id=peer, device_id_type=MESH)
 
@@ -395,71 +399,75 @@
     part[...] = lax.dot_general(
         sums_high, error, dims, preferred_element_type=F32
     ) + lax.dot_general(sums_low, error, dims, preferred_element_type=F32)
-    theirs = pl.multiple_of((1 - c) * 128, 128)
-    mine = pl.multiple_of(c * 128, 128)
-    first = copy(part.at[pl.ds(theirs, 128)], a1r, sibling)
+    part_low[...] = part[...].astype(BF16)
+    board = c * NX + x
+    first = Batch(board_in.at[pl.ds(0, 7)], board_peer(0, 1))
+    for d, e in BOARD:
+        at = pl.multiple_of(board_index(d, e) * 32, 32)
+        first.start(part_low.at[pl.ds(at, 32)], board_in.at[d * NX + e], board_peer(d, e))
     for one in earlier:
         one.wait_send()
     relay(1, 0, state)
     forward(1, 1, state)
 
-    first.wait_recv()
-    half[...] = part[pl.ds(mine, 128), :] + a1r[...]
-    a2s[...] = half[...].astype(BF16)
-    second = Batch(a2r.at[pl.ds(1, NY - 1)], y_peer(1))
-    for e in range(1, NY):
-        at = pl.multiple_of(((y + e) % NY) * 16, 16)
-        second.start(a2s.at[pl.ds(at, 16)], a2r.at[e], y_peer(e))
-
     forward_t(1, state)
     forward(1, 2, state)
     relay(1, 1, state)
+
+    first.wait_recv()
+    piece = part[pl.ds(pl.multiple_of(board * 32, 32), 32), :]
+    for d, e in BOARD:
+        piece = piece + board_in[d * NX + e].astype(F32)
+    for n in range(NY):
+        tiles[n] = piece[n // 2 * 8:n // 2 * 8 + 8, n % 2 * HALF:(n % 2 + 1) * HALF]
+    second = Batch(tiles_in.at[pl.ds(1, NY - 1)], y_peer(1))
+    for e in range(1, NY):
+        second.start(tiles.at[(y + e) % NY], tiles_in.at[e], y_peer(e))
+
     near_first(1, state)
-
-    piece = half[pl.ds(pl.multiple_of(y * 16, 16), 16), :]
-    second.wait_recv()
-    for e in range(1, NY):
-        piece = piece + a2r[e].astype(F32)
-    a3r[z] = piece.astype(BF16)
-    third = Batch(a3r.at[pl.ds(0, NZ - 1)], z_peer(1))
-    for e in range(1, NZ):
-        third.start(a3r.at[z], a3r.at[z], z_peer(e))
-
     relay(1, 2, state)
     near_second(1)
+
+    second.wait_recv()
+    tile = tiles[y]
+    for e in range(1, NY):
+        tile = tile + tiles_in[e]
+    ring[z] = tile
+    third = Batch(ring.at[pl.ds(0, NZ - 1)], z_peer(1))
+    for e in range(1, NZ):
+        third.start(ring.at[z], ring.at[z], z_peer(e))
+
     next_first(1, state)
     finish_gather(state)
     sums_first(1, state)
 
     third.wait_recv()
-    piece = a3r[0].astype(F32)
+    tile = ring[0]
     for n in range(1, NZ):
-        piece = piece + a3r[n].astype(F32)
-    a4r[x] = piece
-    fourth = Batch(a4r.at[pl.ds(0, NX - 1)], x_peer(1))
-    for e in range(1, NX):
-        fourth.start(a4r.at[x], a4r.at[x], x_peer(e))
+        tile = tile + ring[n]
+    whole[y] = tile
+    fourth = Batch(whole.at[pl.ds(0, NY - 1)], y_peer(1))
+    for e in range(1, NY):
+        fourth.start(whole.at[y], whole.at[y], y_peer(e))
 
     next_own(1, state)
     product(1, 1)
+    sums_second(1, state)
     next_second(1, state)
 
     fourth.wait_recv()
-    piece = (a4r[0] + a4r[1]) + (a4r[2] + a4r[3])
-    at = pl.multiple_of(c * 128 + y * 16, 16)
-    wbuf[pl.ds(at, 16), :] = piece.astype(BF16)
-    fifth = Batch(wbuf.at[pl.ds(0, 16 * (NY - 1))], y_peer(1))
-    for e in range(1, NY):
-        fifth.start(wbuf.at[pl.ds(at, 16)], wbuf.at[pl.ds(at, 16)], y_peer(e))
-    sums_second(1, state)
-    fifth.wait_recv()
-    sixth = copy(wbuf.at[pl.ds(mine, 128)], wbuf.at[pl.ds(mine, 128)], sibling)
+    rows = [jnp.concatenate([whole[2 * n], whole[2 * n + 1]], axis=1) for n in range(4)]
+    run = pl.ds(pl.multiple_of(board * 32, 32), 32)
+    wbuf[run, :] = jnp.concatenate(rows, axis=0).astype(BF16)
+    fifth = Batch(wbuf.at[pl.ds(0, 7 * 32)], board_peer(0, 1))
+    for d, e in BOARD:
+        fifth.start(wbuf.at[run], wbuf.at[run], board_peer(d, e))
     back = jnp.concatenate([sums_last(1, state), sums_last_t(1, state)], axis=1)
     vgrad = (scale * back).astype(BF16)
     grad_feats[...] = lax.dot_general(
         vgrad, weight[...], (((1,), (1,)), ((), ())), preferred_element_type=F32
     ).astype(BF16)
-    sixth.wait_recv()
+    fifth.wait_recv()
     grad_weight[...] = wbuf[...].astype(F32)
     for one in started[len(earlier):]:
         one.wait_send()
@@ -513,12 +521,12 @@
             pltpu.VMEM((8, 16, 512), F32),
             pltpu.VMEM((NX, 2, 8, 512), F32),
             pltpu.VMEM((256, 256), F32),
-            pltpu.VMEM((128, 256), F32),
-            pltpu.VMEM((128, 256), F32),
-            pltpu.VMEM((128, 256), BF16),
-            pltpu.VMEM((NY, 16, 256), BF16),
-            pltpu.VMEM((NZ, 16, 256), BF16),
-            pltpu.VMEM((NX, 16, 256), F32),
+            pltpu.VMEM((256, 256), BF16),
+            pltpu.VMEM((2 * NX, 32, 256), BF16),
+            pltpu.VMEM((NY, 8, HALF), F32),
+            pltpu.VMEM((NY, 8, HALF), F32),
+            pltpu.VMEM((NZ, 8, HALF), F32),
+            pltpu.VMEM((NY, 8, HALF), F32),
             pltpu.VMEM((256, 256), BF16),
             pltpu.VMEM((ROWS, 256), F32),
             pltpu.SemaphoreType.DMA((COPIES,)),

time: 68 us -> 69 us (1.015)
  Pallas kernels: 67.3 us -> 68.3 us
    pallas_call x1, Pallas kernels: 66.5 us -> 67.5 us  [local(): pl.pallas_call(functools.partial(kernel, coef), out_shape=tuple((pltpu.VM...]
where the time goes in v7:
time: 69 us; the launch traced here: 68.9 us
  Pallas kernels  68.3 us (99%)
    pallas_call x1, Pallas kernels, local(): pl.pallas_call(functools.partial(kernel, coef), out_shape=tuple((pltpu.VM...  67.5 us

profile of v7, /device:TPU:1, one launch (start us, length us, event | category | flops | bytes accessed | tf_op | source)
XLA Modules:
  0.0 68.9 jit_solution(14733950903887641072)
XLA Ops:
  0.6 67.5 %shard_map.76 = (bf16[64,256]{1,0:T(8,128)(2,1)S(1)}, bf16[64,256]{1,0:T(8,128)(2,1)S(1)}, f32[256,256]{1,0:T(8,128)S(1)}) custom-call(bf16[64,256]{1,0:T(8,128)(2,1)} %feats_hbm.1, bf16[256,256]{1,0:T(8,128)(2,1)} %weight_hbm.1, bf16[1,64]{1,0:T(2,128)(2,1)} %bitcast.1, s32[2,256]{1,0:T(2,128)} %mask_hbm.1, bf16[64,256]{1,0:T(8,128)(2,1)} %cot_hbm.1), custom_call_target="tpu_custom_call" | custom-call | tf_op jit(solution)/shard_map/pallas_call | solution.py:491
  68.2 0.8 %shard_map.77 = (bf16[64,256]{1,0:T(8,128)(2,1)}, bf16[64,256]{1,0:T(8,128)(2,1)}, f32[256,256]{1,0:T(8,128)}) custom-call(bf16[64,256]{1,0:T(8,128)(2,1)S(1)} %get-tuple-element.6.refs_0_, bf16[64,256]{1,0:T(8,128)(2,1)S(1)} %get-tuple-element.7.refs_1_, f32[256,256]{1,0:T(8,128)S(1)} %get-tuple-element.8.refs_2_), custom_call_target="tpu_custom_call" | custom-call | tf_op jit(solution)/shard_map/pallas_call | solution.py:539

commit v8 on v5

--- a/solution.py
+++ b/solution.py
@@ -46,7 +46,7 @@
     feats, weight, scale_row, mask, cot, load_sems,
     adj, cm, gath, gath_t, masks, csend, crecv, acc, ysend, yrecv,
     near_send, near_recv, keep, keep_near, next_send, next_recv, zsend, zrecv,
-    starts, steps, part, a1r, half, a2s, a2r, a3r, a4r, wbuf, scale_col,
+    begun, begun_t, starts, steps, part, a1r, half, a2s, a2r, a3r, a4r, wbuf, scale_col,
     send_sems, recv_sems,
 ):
     sec = lax.axis_index("section")
@@ -250,17 +250,18 @@
         for one in state["opp"]:
             one.wait_recv()
 
-    def product(p, side):
+    def early(p):
+        right = gath[p, 0:3].reshape(3 * NZ * ROWS, HALF)
+        begun[...] = jnp.dot(adj[0:512, 0:1536], right, preferred_element_type=F32)
+
+    def sums_first(p, state):
+        rest = jnp.dot(adj[0:512, 1536:2048], gath[p, 3], preferred_element_type=F32)
+        csend[p] = (begun[...] + rest).astype(BF16)
+        state["core"] = copy(csend.at[p], crecv.at[p], sibling)
+
+    def product(p):
         right = gath[p].reshape(NX * NZ * ROWS, HALF)
-        value = jnp.dot(adj[side * 512:(side + 1) * 512, :], right, preferred_element_type=F32)
-        if side == 0:
-            csend[p] = value.astype(BF16)
-        else:
-            acc[...] = value
-
-    def sums_first(p, state):
-        product(p, 0)
-        state["core"] = copy(csend.at[p], crecv.at[p], sibling)
+        acc[...] = jnp.dot(adj[512:1024, :], right, preferred_element_type=F32)
 
     def sums_second(p, state):
         state["core"].wait_recv()
@@ -279,14 +280,19 @@
             total = total + yrecv[p, e].astype(F32)
         return total
 
+    def early_t(p):
+        for n in range(NX):
+            lanes = slice(n * 512, (n + 1) * 512)
+            begun_t[:, lanes] = lax.dot_general(
+                gath_t[p, 0], adj[512:1024, lanes], (((0,), (0,)), ((), ())),
+                preferred_element_type=F32,
+            )
+
     def product_t(p, lo, hi):
-        dims = (((0,), (0,)), ((), ()))
-        turned = lax.dot_general(
-            gath_t[p, 1], adj[0:512, lo:hi], dims, preferred_element_type=F32
-        ) + lax.dot_general(
-            gath_t[p, 0], adj[512:1024, lo:hi], dims, preferred_element_type=F32
+        rest = lax.dot_general(
+            gath_t[p, 1], adj[0:512, lo:hi], (((0,), (0,)), ((), ())), preferred_element_type=F32
         )
-        return turned.T
+        return (begun_t[:, lo:hi] + rest).T
 
     def near_first(p, state):
         for one in state["core_t"]:
@@ -347,27 +353,29 @@
     prepare_block()
     mask_copies.wait_recv()
     mask_columns()
-    make_block(3, 0)
+    make_block(3, 1)
     relay(0, 0, state)
-    make_block(3, 1)
+    make_block(1, 1)
     forward(0, 1, state)
-    make_block(1, 0)
-    make_block(1, 1)
+    make_block(2, 1)
+    make_block(0, 1)
     forward_t(0, state)
     forward(0, 2, state)
     relay(0, 1, state)
+    make_block(3, 0)
+    early_t(0)
+    make_block(1, 0)
     make_block(2, 0)
-    make_block(2, 1)
     near_first(0, state)
     relay(0, 2, state)
     near_second(0)
     make_block(0, 0)
-    make_block(0, 1)
+    early(0)
     next_first(0, state)
     finish_gather(state)
     sums_first(0, state)
     next_own(0, state)
-    product(0, 1)
+    product(0)
     next_second(0, state)
     sums_second(0, state)
     sums = jnp.concatenate([sums_last(0, state), sums_last_t(0, state)], axis=1)
@@ -414,6 +422,7 @@
     forward_t(1, state)
     forward(1, 2, state)
     relay(1, 1, state)
+    early_t(1)
     near_first(1, state)
 
     piece = half[pl.ds(pl.multiple_of(y * 16, 16), 16), :]
@@ -427,6 +436,7 @@
 
     relay(1, 2, state)
     near_second(1)
+    early(1)
     next_first(1, state)
     finish_gather(state)
     sums_first(1, state)
@@ -441,7 +451,7 @@
         fourth.start(a4r.at[x], a4r.at[x], x_peer(e))
 
     next_own(1, state)
-    product(1, 1)
+    product(1)
     next_second(1, state)
 
     fourth.wait_recv()
@@ -510,6 +520,8 @@
             pltpu.VMEM((2, 2, 256, HALF), BF16),
             pltpu.VMEM((2, 512, HALF), BF16),
             pltpu.VMEM((2, NZ, ROWS, HALF), BF16),
+            pltpu.VMEM((512, HALF), F32),
+            pltpu.VMEM((HALF, 2048), F32),
             pltpu.VMEM((8, 16, 512), F32),
             pltpu.VMEM((NX, 2, 8, 512), F32),
             pltpu.VMEM((256, 256), F32),

time: 68 us -> 67.1 us (0.987)
  Pallas kernels: 67.3 us -> 66.3 us
    pallas_call x1, Pallas kernels: 66.5 us -> 65.6 us  [local(): pl.pallas_call(functools.partial(kernel, coef), out_shape=tuple((pltpu.VM...]
where the time goes in v8:
time: 67.1 us; the launch traced here: 67 us
  Pallas kernels  66.3 us (99%)
    pallas_call x1, Pallas kernels, local(): pl.pallas_call(functools.partial(kernel, coef), out_shape=tuple((pltpu.VM...  65.6 us

profile of v8, /device:TPU:1, one launch (start us, length us, event | category | flops | bytes accessed | tf_op | source)
XLA Modules:
  0.0 67.0 jit_solution(5783655734153730880)
XLA Ops:
  0.6 65.6 %shard_map.76 = (bf16[64,256]{1,0:T(8,128)(2,1)S(1)}, bf16[64,256]{1,0:T(8,128)(2,1)S(1)}, f32[256,256]{1,0:T(8,128)S(1)}) custom-call(bf16[64,256]{1,0:T(8,128)(2,1)} %feats_hbm.1, bf16[256,256]{1,0:T(8,128)(2,1)} %weight_hbm.1, bf16[1,64]{1,0:T(2,128)(2,1)} %bitcast.1, s32[2,256]{1,0:T(2,128)} %mask_hbm.1, bf16[64,256]{1,0:T(8,128)(2,1)} %cot_hbm.1), custom_call_target="tpu_custom_call" | custom-call | tf_op jit(solution)/shard_map/pallas_call | solution.py:493
  66.2 0.8 %shard_map.77 = (bf16[64,256]{1,0:T(8,128)(2,1)}, bf16[64,256]{1,0:T(8,128)(2,1)}, f32[256,256]{1,0:T(8,128)}) custom-call(bf16[64,256]{1,0:T(8,128)(2,1)S(1)} %get-tuple-element.6.refs_0_, bf16[64,256]{1,0:T(8,128)(2,1)S(1)} %get-tuple-element.7.refs_1_, f32[256,256]{1,0:T(8,128)S(1)} %get-tuple-element.8.refs_2_), custom_call_target="tpu_custom_call" | custom-call | tf_op jit(solution)/shard_map/pallas_call | solution.py:543

commit v9 on v8

--- a/solution.py
+++ b/solution.py
@@ -300,9 +300,12 @@
         opposite = product_t(p, 1536, 2048)
         near_send[p, 0, 256:512] = opposite[:256].astype(BF16)
         near_send[p, 1, 256:512] = opposite[256:].astype(BF16)
-        far, close = pl.ds(256, 256), pl.ds(0, 256)
+        far = pl.ds(256, 256)
         state["far_e"] = copy(near_send.at[p, 0, far], near_recv.at[p, 0, far], east)
         state["far_w"] = copy(near_send.at[p, 1, far], near_recv.at[p, 1, far], west)
+
+    def near_close(p, state):
+        close = pl.ds(0, 256)
         near_send[p, 0, 0:256] = product_t(p, 512, 768).astype(BF16)
         state["near_e"] = copy(near_send.at[p, 0, close], near_recv.at[p, 0, close], east)
         near_send[p, 1, 0:256] = product_t(p, 1280, 1536).astype(BF16)
@@ -368,6 +371,7 @@
     make_block(2, 0)
     near_first(0, state)
     relay(0, 2, state)
+    near_close(0, state)
     near_second(0)
     make_block(0, 0)
     early(0)
@@ -424,6 +428,8 @@
     relay(1, 1, state)
     early_t(1)
     near_first(1, state)
+    relay(1, 2, state)
+    near_close(1, state)
 
     piece = half[pl.ds(pl.multiple_of(y * 16, 16), 16), :]
     second.wait_recv()
@@ -434,7 +440,6 @@
     for e in range(1, NZ):
         third.start(a3r.at[z], a3r.at[z], z_peer(e))
 
-    relay(1, 2, state)
     near_second(1)
     early(1)
     next_first(1, state)

time: 67.1 us -> 67.6 us (level)
  no operation moved by 1% of the time
where the time goes in v9:
time: 67.6 us; the launch traced here: 67.5 us
  Pallas kernels  66.8 us (99%)
    pallas_call x1, Pallas kernels, local(): pl.pallas_call(functools.partial(kernel, coef), out_shape=tuple((pltpu.VM...  66.1 us

profile of v9, /device:TPU:1, one launch (start us, length us, event | category | flops | bytes accessed | tf_op | source)
XLA Modules:
  0.0 67.5 jit_solution(5672274563354828316)
XLA Ops:
  0.6 66.1 %shard_map.76 = (bf16[64,256]{1,0:T(8,128)(2,1)S(1)}, bf16[64,256]{1,0:T(8,128)(2,1)S(1)}, f32[256,256]{1,0:T(8,128)S(1)}) custom-call(bf16[64,256]{1,0:T(8,128)(2,1)} %feats_hbm.1, bf16[256,256]{1,0:T(8,128)(2,1)} %weight_hbm.1, bf16[1,64]{1,0:T(2,128)(2,1)} %bitcast.1, s32[2,256]{1,0:T(2,128)} %mask_hbm.1, bf16[64,256]{1,0:T(8,128)(2,1)} %cot_hbm.1), custom_call_target="tpu_custom_call" | custom-call | tf_op jit(solution)/shard_map/pallas_call | solution.py:498
  66.7 0.8 %shard_map.77 = (bf16[64,256]{1,0:T(8,128)(2,1)}, bf16[64,256]{1,0:T(8,128)(2,1)}, f32[256,256]{1,0:T(8,128)}) custom-call(bf16[64,256]{1,0:T(8,128)(2,1)S(1)} %get-tuple-element.6.refs_0_, bf16[64,256]{1,0:T(8,128)(2,1)S(1)} %get-tuple-element.7.refs_1_, f32[256,256]{1,0:T(8,128)S(1)} %get-tuple-element.8.refs_2_), custom_call_target="tpu_custom_call" | custom-call | tf_op jit(solution)/shard_map/pallas_call | solution.py:548

commit v10 on v8

--- a/solution.py
+++ b/solution.py
@@ -213,14 +213,14 @@
         for g, (lo, hi) in enumerate(GROUPS[1:], 1):
             state["z"][g] = Batch(gath.at[p, 0, pl.ds(lo * ROWS, (hi - lo) * ROWS)], z_peer(1))
         state["y_t"] = Batch(gath_t.at[p, 0, pl.ds(ROWS, (NY - 1) * ROWS)], y_peer(1))
+        for k in (7, 6, 5, 4, 3, 2, 1):
+            e = (NY - OFFSET[k]) % NY
+            state["y_t"].start(own_t, gath_t.at[p, 0, pl.ds(k * ROWS, ROWS)], y_peer(e))
         for k in range(1, NZ):
             e = (NZ - OFFSET[k]) % NZ
             g = 1 if k < GROUPS[1][1] else 2
             state["z"][g].start(own, gath.at[p, 0, pl.ds(k * ROWS, ROWS)], z_peer(e))
-            far = NY - k
-            e = (NY - OFFSET[far]) % NY
-            state["y_t"].start(own_t, gath_t.at[p, 0, pl.ds(far * ROWS, ROWS)], y_peer(e))
-            if k == 2:
+            if k == 4:
                 forward(p, 0, state)
         return state
 

time: 67.1 us -> 67.2 us (level)
  no operation moved by 1% of the time
where the time goes in v10:
time: 67.2 us; the launch traced here: 67 us
  Pallas kernels  66.4 us (99%)
    pallas_call x1, Pallas kernels, local(): pl.pallas_call(functools.partial(kernel, coef), out_shape=tuple((pltpu.VM...  65.6 us

profile of v10, /device:TPU:1, one launch (start us, length us, event | category | flops | bytes accessed | tf_op | source)
XLA Modules:
  0.0 67.0 jit_solution(5313845258866690823)
XLA Ops:
  0.6 65.6 %shard_map.76 = (bf16[64,256]{1,0:T(8,128)(2,1)S(1)}, bf16[64,256]{1,0:T(8,128)(2,1)S(1)}, f32[256,256]{1,0:T(8,128)S(1)}) custom-call(bf16[64,256]{1,0:T(8,128)(2,1)} %feats_hbm.1, bf16[256,256]{1,0:T(8,128)(2,1)} %weight_hbm.1, bf16[1,64]{1,0:T(2,128)(2,1)} %bitcast.1, s32[2,256]{1,0:T(2,128)} %mask_hbm.1, bf16[64,256]{1,0:T(8,128)(2,1)} %cot_hbm.1), custom_call_target="tpu_custom_call" | custom-call | tf_op jit(solution)/shard_map/pallas_call | solution.py:493
  66.3 0.8 %shard_map.77 = (bf16[64,256]{1,0:T(8,128)(2,1)}, bf16[64,256]{1,0:T(8,128)(2,1)}, f32[256,256]{1,0:T(8,128)}) custom-call(bf16[64,256]{1,0:T(8,128)(2,1)S(1)} %get-tuple-element.6.refs_0_, bf16[64,256]{1,0:T(8,128)(2,1)S(1)} %get-tuple-element.7.refs_1_, f32[256,256]{1,0:T(8,128)S(1)} %get-tuple-element.8.refs_2_), custom_call_target="tpu_custom_call" | custom-call | tf_op jit(solution)/shard_map/pallas_call | solution.py:543

commit v11 on v10

--- a/solution.py
+++ b/solution.py
@@ -206,7 +206,7 @@
 
     pl.semaphore_wait(barrier, len(peers))
 
-    def start_pass(p):
+    def start_pass(p, between):
         own = gath.at[p, 0, pl.ds(0, ROWS)]
         own_t = gath_t.at[p, 0, pl.ds(0, ROWS)]
         state = {"z": {}, "one": {}, "two": {}, "opp": [], "y_t": {}, "core_t": []}
@@ -216,6 +216,7 @@
         for k in (7, 6, 5, 4, 3, 2, 1):
             e = (NY - OFFSET[k]) % NY
             state["y_t"].start(own_t, gath_t.at[p, 0, pl.ds(k * ROWS, ROWS)], y_peer(e))
+        between()
         for k in range(1, NZ):
             e = (NZ - OFFSET[k]) % NZ
             g = 1 if k < GROUPS[1][1] else 2
@@ -347,9 +348,12 @@
         return total
 
     mask_copies = Batch(masks.at[pl.ds(0, NZ - 1)], z_peer(1))
-    for e in range(1, NZ):
-        mask_copies.start(masks.at[z], masks.at[z], z_peer(e))
-    state = start_pass(0)
+
+    def send_mask():
+        for e in range(1, NZ):
+            mask_copies.start(masks.at[z], masks.at[z], z_peer(e))
+
+    state = start_pass(0, send_mask)
     prepare_block()
     mask_copies.wait_recv()
     mask_columns()
@@ -385,20 +389,27 @@
     sums_high = sums.astype(BF16)
     sums_low = (sums - sums_high.astype(F32)).astype(BF16)
     scale = scale_col[...]
-    presum = scale * (
-        jnp.dot(sums_high, weight[...], preferred_element_type=F32)
-        + jnp.dot(sums_low, weight[...], preferred_element_type=F32)
-    )
-    sigma = jax.nn.sigmoid(presum)
-    layer_out[...] = (presum * sigma).astype(BF16)
-    deriv = sigma * (1.0 + presum * (1.0 - sigma))
-    error = (scale * cot[...].astype(F32) * deriv).astype(BF16)
-    gath[1, 0, 0:ROWS] = error[:, :HALF]
-    gath_t[1, 0, 0:ROWS] = error[:, HALF:]
+
+    def error_half(f):
+        lanes = slice(f * HALF, (f + 1) * HALF)
+        presum = scale[:, lanes] * (
+            jnp.dot(sums_high, weight[:, lanes], preferred_element_type=F32)
+            + jnp.dot(sums_low, weight[:, lanes], preferred_element_type=F32)
+        )
+        sigma = jax.nn.sigmoid(presum)
+        layer_out[:, lanes] = (presum * sigma).astype(BF16)
+        deriv = sigma * (1.0 + presum * (1.0 - sigma))
+        return (scale[:, lanes] * cot[:, lanes].astype(F32) * deriv).astype(BF16)
+
+    gath_t[1, 0, 0:ROWS] = error_half(1)
+
+    def first_half():
+        gath[1, 0, 0:ROWS] = error_half(0)
 
     earlier = list(started)
 
-    state = start_pass(1)
+    state = start_pass(1, first_half)
+    error = jnp.concatenate([gath[1, 0, 0:ROWS], gath_t[1, 0, 0:ROWS]], axis=1)
     dims = (((0,), (0,)), ((), ()))
     part[...] = lax.dot_general(
         sums_high, error, dims, preferred_element_type=F32

time: 67.2 us -> 67.5 us (level)
  no operation moved by 1% of the time
where the time goes in v11:
time: 67.5 us; the launch traced here: 67.3 us
  Pallas kernels  66.7 us (99%)
    pallas_call x1, Pallas kernels, local(): pl.pallas_call(functools.partial(kernel, coef), out_shape=tuple((pltpu.VM...  65.9 us

profile of v11, /device:TPU:1, one launch (start us, length us, event | category | flops | bytes accessed | tf_op | source)
XLA Modules:
  0.0 67.3 jit_solution(4511400923817248837)
XLA Ops:
  0.6 65.9 %shard_map.76 = (bf16[64,256]{1,0:T(8,128)(2,1)S(1)}, bf16[64,256]{1,0:T(8,128)(2,1)S(1)}, f32[256,256]{1,0:T(8,128)S(1)}) custom-call(bf16[64,256]{1,0:T(8,128)(2,1)} %feats_hbm.1, bf16[256,256]{1,0:T(8,128)(2,1)} %weight_hbm.1, bf16[1,64]{1,0:T(2,128)(2,1)} %bitcast.1, s32[2,256]{1,0:T(2,128)} %mask_hbm.1, bf16[64,256]{1,0:T(8,128)(2,1)} %cot_hbm.1), custom_call_target="tpu_custom_call" | custom-call | tf_op jit(solution)/shard_map/pallas_call | solution.py:504
  66.6 0.8 %shard_map.77 = (bf16[64,256]{1,0:T(8,128)(2,1)}, bf16[64,256]{1,0:T(8,128)(2,1)}, f32[256,256]{1,0:T(8,128)}) custom-call(bf16[64,256]{1,0:T(8,128)(2,1)S(1)} %get-tuple-element.6.refs_0_, bf16[64,256]{1,0:T(8,128)(2,1)S(1)} %get-tuple-element.7.refs_1_, f32[256,256]{1,0:T(8,128)S(1)} %get-tuple-element.8.refs_2_), custom_call_target="tpu_custom_call" | custom-call | tf_op jit(solution)/shard_map/pallas_call | solution.py:554

commit v12 on v10

--- a/solution.py
+++ b/solution.py
@@ -453,6 +453,7 @@
     next_own(1, state)
     product(1)
     next_second(1, state)
+    sums_second(1, state)
 
     fourth.wait_recv()
     piece = (a4r[0] + a4r[1]) + (a4r[2] + a4r[3])
@@ -461,7 +462,6 @@
     fifth = Batch(wbuf.at[pl.ds(0, 16 * (NY - 1))], y_peer(1))
     for e in range(1, NY):
         fifth.start(wbuf.at[pl.ds(at, 16)], wbuf.at[pl.ds(at, 16)], y_peer(e))
-    sums_second(1, state)
     fifth.wait_recv()
     sixth = copy(wbuf.at[pl.ds(mine, 128)], wbuf.at[pl.ds(mine, 128)], sibling)
     back = jnp.concatenate([sums_last(1, state), sums_last_t(1, state)], axis=1)

time: 67.2 us -> 67.5 us (level)
  no operation moved by 1% of the time
where the time goes in v12:
time: 67.5 us; the launch traced here: 67.4 us
  Pallas kernels  66.7 us (99%)
    pallas_call x1, Pallas kernels, local(): pl.pallas_call(functools.partial(kernel, coef), out_shape=tuple((pltpu.VM...  66 us

profile of v12, /device:TPU:1, one launch (start us, length us, event | category | flops | bytes accessed | tf_op | source)
XLA Modules:
  0.0 67.4 jit_solution(12926927943991977961)
XLA Ops:
  0.6 66.0 %shard_map.76 = (bf16[64,256]{1,0:T(8,128)(2,1)S(1)}, bf16[64,256]{1,0:T(8,128)(2,1)S(1)}, f32[256,256]{1,0:T(8,128)S(1)}) custom-call(bf16[64,256]{1,0:T(8,128)(2,1)} %feats_hbm.1, bf16[256,256]{1,0:T(8,128)(2,1)} %weight_hbm.1, bf16[1,64]{1,0:T(2,128)(2,1)} %bitcast.1, s32[2,256]{1,0:T(2,128)} %mask_hbm.1, bf16[64,256]{1,0:T(8,128)(2,1)} %cot_hbm.1), custom_call_target="tpu_custom_call" | custom-call | tf_op jit(solution)/shard_map/pallas_call | solution.py:493
  66.6 0.8 %shard_map.77 = (bf16[64,256]{1,0:T(8,128)(2,1)}, bf16[64,256]{1,0:T(8,128)(2,1)}, f32[256,256]{1,0:T(8,128)}) custom-call(bf16[64,256]{1,0:T(8,128)(2,1)S(1)} %get-tuple-element.6.refs_0_, bf16[64,256]{1,0:T(8,128)(2,1)S(1)} %get-tuple-element.7.refs_1_, f32[256,256]{1,0:T(8,128)S(1)} %get-tuple-element.8.refs_2_), custom_call_target="tpu_custom_call" | custom-call | tf_op jit(solution)/shard_map/pallas_call | solution.py:543
